TPU v7x, 32 devices: a whole 2x2x4 slice. The times are simulated.
32 devices in a mesh: obs: 8 (over y, x, core), row: 4 (over z).
Axes of the slice: x: 2, y: 2, z: 4, core: 2. Of those that a mesh axis runs over, the one named last changes fastest.
Arguments:
- camera_jacobian: float32 [18, 32768], P(None, ('obs', 'row')), may hold values from -0.75 to 0.75
- point_jacobian: float32 [6, 32768], P(None, ('obs', 'row')), may hold values from -6 to 6
- residual: float32 [2, 32768], P(None, ('obs', 'row')), may hold values from -6 to 6
- send_order: int32 [32768], P(('obs', 'row')), may hold values from 0 to 1023, as said below
- camera_of: int32 [32768], P(('obs', 'row')), may hold values from 0 to 63, as said below
- track_of: int32 [32768], P(('obs', 'row')), may hold values from 0 to 511, as said below
- partner: int32 [7, 32768], P(None, ('obs', 'row')), may hold values from 0 to 1023, as said below
- pair_slot: int32 [7, 32768], P(None, ('obs', 'row')), may hold values from 0 to 896, as said below
Outputs:
- camera_hessian: float32 [81, 512], P(None, ('obs', 'row'))
- camera_gradient: float32 [9, 512], P(None, ('obs', 'row'))
- pair_hessian: float32 [81, 7168], P(None, ('obs', 'row'))
Inputs may be any that keep to these rules, and one draw needn't show every extreme that they name: `send_order`: on each device a permutation of the device's 1024 observations. `camera_of`: A device's observations are ordered by camera. `track_of`: local track of each received slot of one track owner; a track has 2 to 8 observations, at most one from each source obs index, from cyclically consecutive source obs indices; some track ids are unused. partner[k] of a received slot is the slot of the k-th other observation of its track in track order, or the slot itself where the track has fewer than k + 2 observations. pair_slot[k] of a send slot is c * 14 + o, where c is the observation's camera and o encodes its partner's camera; 896 exactly where partner[k] is the slot itself.
All inputs are finite; a program needn't handle non-finite values.
Results may differ from a plain program's by a relative error of at most 0.00014.
Values sent between devices are 32-bit elements; how exact they have to be, the bound alone decides.
A program may use at most 64 MiB of HBM per device.

v0:
```python
import jax
import jax.numpy as jnp
from jax import lax
from jax.sharding import PartitionSpec as P

CAM_ROW = 16
NBR = 14


damping = 1.0


def eliminate(camera_rows, point_rows, resid_rows, track_of, track_count):
    camera = camera_rows.reshape(2, 9, -1)
    point_jac = point_rows.reshape(2, 3, -1)
    normal = jnp.stack(
        [
            point_jac[0, 0] * point_jac[0, 0] + point_jac[1, 0] * point_jac[1, 0],
            point_jac[0, 0] * point_jac[0, 1] + point_jac[1, 0] * point_jac[1, 1],
            point_jac[0, 0] * point_jac[0, 2] + point_jac[1, 0] * point_jac[1, 2],
            point_jac[0, 1] * point_jac[0, 1] + point_jac[1, 1] * point_jac[1, 1],
            point_jac[0, 1] * point_jac[0, 2] + point_jac[1, 1] * point_jac[1, 2],
            point_jac[0, 2] * point_jac[0, 2] + point_jac[1, 2] * point_jac[1, 2],
            point_jac[0, 0] * resid_rows[0] + point_jac[1, 0] * resid_rows[1],
            point_jac[0, 1] * resid_rows[0] + point_jac[1, 1] * resid_rows[1],
            point_jac[0, 2] * resid_rows[0] + point_jac[1, 2] * resid_rows[1],
        ]
    )
    totals = jnp.zeros((9, track_count), jnp.float32).at[:, track_of].add(normal)
    pivot_first = jnp.sqrt(totals[0] + damping)
    lower_one = totals[1] / pivot_first
    lower_two = totals[2] / pivot_first
    pivot_second = jnp.sqrt(totals[3] + damping - lower_one * lower_one)
    lower_mid = (totals[4] - lower_two * lower_one) / pivot_second
    pivot_third = jnp.sqrt(totals[5] + damping - lower_two * lower_two - lower_mid * lower_mid)
    solved_one = totals[6] / pivot_first
    solved_two = (totals[7] - lower_one * solved_one) / pivot_second
    solved_three = (totals[8] - lower_two * solved_one - lower_mid * solved_two) / pivot_third
    per_track = jnp.stack(
        [
            pivot_first,
            lower_one,
            lower_two,
            pivot_second,
            lower_mid,
            pivot_third,
            solved_one,
            solved_two,
            solved_three,
        ]
    )
    per_obs = per_track[:, track_of]
    weights = (
        camera[0][:, None, :] * point_jac[0][None, :, :]
        + camera[1][:, None, :] * point_jac[1][None, :, :]
    )
    column_one = weights[:, 0] / per_obs[0]
    column_two = (weights[:, 1] - per_obs[1] * column_one) / per_obs[3]
    column_three = (weights[:, 2] - per_obs[2] * column_one - per_obs[4] * column_two) / per_obs[5]
    factor = jnp.stack([column_one, column_two, column_three])
    point_shift = column_one * per_obs[6] + column_two * per_obs[7] + column_three * per_obs[8]
    return (factor, point_shift)


def camera_terms(camera_rows, resid_rows, factor, point_shift):
    camera = camera_rows.reshape(2, 9, -1)
    normal = (
        camera[0][:, None, :] * camera[0][None, :, :]
        + camera[1][:, None, :] * camera[1][None, :, :]
    )
    schur_part = (
        factor[0][:, None, :] * factor[0][None, :, :]
        + factor[1][:, None, :] * factor[1][None, :, :]
        + factor[2][:, None, :] * factor[2][None, :, :]
    )
    gradient = camera[0] * resid_rows[0] + camera[1] * resid_rows[1] - point_shift
    return jnp.concatenate([(normal - schur_part).reshape(81, -1), gradient], axis=0)


def pair_product(left, right):
    total = (
        left[0][:, None] * right[0][None, :]
        + left[1][:, None] * right[1][None, :]
        + left[2][:, None] * right[2][None, :]
    )
    return -total.reshape(81, -1)


def on_device(
    camera_jacobian, point_jacobian, residual, send_order, camera_of, track_of, partner, pair_slot
):
    obs_count = camera_jacobian.shape[1]
    ranks = partner.shape[0]
    camera_count = CAM_ROW * lax.axis_size("row")
    slot_count = camera_count * NBR
    stacked = jnp.concatenate([camera_jacobian, point_jacobian, residual], axis=0)
    sent = jnp.take(stacked, send_order, axis=1)
    owned = lax.all_to_all(sent, "obs", split_axis=1, concat_axis=1, tiled=True)
    factor, point_shift = eliminate(
        owned[:18], owned[18:24], owned[24:26], track_of, obs_count // 2
    )
    flat_factor = factor.reshape(27, obs_count)
    chosen = jnp.take(flat_factor, partner.reshape(-1), axis=1)
    together = jnp.concatenate(
        [
            flat_factor,
            point_shift,
            chosen.reshape(27, ranks, obs_count).reshape(27 * ranks, obs_count),
        ],
        axis=0,
    )
    back = lax.all_to_all(together, "obs", split_axis=1, concat_axis=1, tiled=True)
    factor_back = back[:27].reshape(3, 9, obs_count)
    shift_back = back[27:36]
    remote = back[36:].reshape(3, 9, ranks, obs_count)
    arrived = pair_product(factor_back[:, :, None, :], remote)
    local_terms = camera_terms(sent[:18], sent[24:26], factor_back, shift_back)
    camera_ids = jnp.take(camera_of, send_order)
    indicator = (camera_ids[:, None] == jnp.arange(camera_count, dtype=jnp.int32)[None, :]).astype(
        jnp.float32
    )
    camera_partial = jnp.dot(
        local_terms, indicator, precision=lax.Precision.HIGHEST, preferred_element_type=jnp.float32
    )
    camera_mine = lax.psum_scatter(camera_partial, "row", scatter_dimension=1, tiled=True)
    pair_total = (
        jnp.zeros((81, slot_count + 1), jnp.float32).at[:, pair_slot.reshape(-1)].add(arrived)
    )
    pair_mine = lax.psum_scatter(pair_total[:, :slot_count], "row", scatter_dimension=1, tiled=True)
    return (camera_mine[:81], camera_mine[81:], pair_mine)


def solution(mesh):
    return jax.shard_map(
        on_device,
        mesh=mesh,
        in_specs=(
            P(None, ("obs", "row")),
            P(None, ("obs", "row")),
            P(None, ("obs", "row")),
            P(("obs", "row")),
            P(("obs", "row")),
            P(("obs", "row")),
            P(None, ("obs", "row")),
            P(None, ("obs", "row")),
        ),
        out_specs=(P(None, ("obs", "row")), P(None, ("obs", "row")), P(None, ("obs", "row"))),
        check_vma=False,
    )
```

profile of v0, /device:TPU:0, one launch (start us, length us, event | category | flops | bytes accessed | tf_op | source)
XLA Modules:
  0.0 166.0 jit_solution(13996789183060499540)
XLA Ops:
  7.2 0.7 fusion.17
  8.0 4.5 %gather_fusion.3 = s32[1024]{0:T(1024)S(1)} fusion(s32[1024]{0:T(1024)S(1)} %copy-done, s32[1024]{0:T(1024)S(1)} %fusion.17), kind=kCustom, calls=%fused_computation.3 | custom fusion | bytes 12288 | tf_op jit(solution)/shard_map/jit(_take)/gather | solution.py:118
  12.8 2.8 %gather_fusion = f32[1024,26]{1,0:T(8,128)S(1)} fusion(f32[26,1024]{0,1:T(8,128)S(1)} %copy.181, s32[1024]{0:T(1024)S(1)} %fusion.17), kind=kCustom, calls=%fused_computation | custom fusion | bytes 217088 | tf_op jit(solution)/shard_map/jit(_take)/gather | solution.py:97
  15.9 0.7 copy_select_fusion
  16.6 5.2 %all-to-all-start = ((f32[26,8,128]{2,0,1:T(8,128)}), f32[26,8,128]{2,0,1:T(8,128)S(1)}, u32[]{:S(2)}, u32[]{:S(2)}) async-start(f32[26,8,128]{2,0,1:T(8,128)} %copy_select_fusion), calls=%async_computation | async-start | bytes 262144 | tf_op jit(solution)/shard_map/all_to_all | solution.py:98
  22.5 4.8 %all-to-all-done = f32[26,8,128]{2,0,1:T(8,128)S(1)} async-done(((f32[26,8,128]{2,0,1:T(8,128)}), f32[26,8,128]{2,0,1:T(8,128)S(1)}, u32[]{:S(2)}, u32[]{:S(2)}) %all-to-all-start) | async-done | bytes 106528 | tf_op jit(solution)/shard_map/all_to_all | solution.py:98
  27.9 6.1 %scatter_custom_fusion = f32[9,512]{0,1:T(8,128)S(1)} fusion(s32[1024]{0:T(1024)S(1)} %get-tuple-element.85, f32[1024,9]{1,0:T(8,128)S(1)} %copy.187, f32[]{:T(128)} %constant.34.clone.1), kind=kCustom, calls=%fused_computation.34 | custom fusion | flops 9216 | bytes 18436 | tf_op jit(solution)/shard_map/scatter-add | solution.py:29
  34.0 0.6 fusion.31
  36.0 2.8 %gather_fusion.1 = f32[1024,9]{1,0:T(8,128)S(1)} fusion(f32[9,512]{0,1:T(8,128)S(1)} %copy.197, s32[1024]{0:T(1024)S(1)} %get-tuple-element.84), kind=kCustom, calls=%fused_computation.1 | custom fusion | bytes 77824 | tf_op jit(solution)/shard_map/gather | solution.py:52
  38.8 2.4 %slice_reduce_fusion.2 = (f32[1024]{0:T(1024)S(1)}, f32[1024]{0:T(1024)S(1)}, f32[1024]{0:T(1024)S(1)}, f32[1024]{0:T(1024)S(1)}, f32[1024]{0:T(1024)S(1)}, /*in...) fusion(f32[9,1024]{0,1:T(8,128)S(1)} %bitcast.164), kind=kLoop, calls=%fused_computation.11 | loop fusion | bytes 73728 | tf_op jit(solution)/shard_map/slice | solution.py:61
  41.6 24.2 %gather_fusion.2 = f32[7168,27]{1,0:T(8,128)} fusion(f32[27,1024]{0,1:T(8,128)S(1)} %copy.198, s32[7168]{0:T(1024)S(1)} %broadcast_clamp_fusion), kind=kCustom, calls=%fused_computation.2 | custom fusion | bytes 1576960 | tf_op jit(solution)/shard_map/jit(_take)/gather | solution.py:103
  65.8 2.6 %copy.199 = f32[27,7168]{1,0:T(8,128)S(1)} copy(f32[27,7168]{0,1:T(8,128)} %bitcast.168) | data formatting | bytes 1548288 | tf_op jit(solution)/shard_map/jit(_take)/gather | solution.py:103
  68.7 1.1 copy.200
  69.8 3.6 %all-to-all-start.1 = ((f32[225,8,128]{2,0,1:T(8,128)}), f32[225,8,128]{2,0,1:T(8,128)S(1)}, u32[]{:S(2)}, u32[]{:S(2)}) async-start(f32[225,8,128]{2,0,1:T(8,128)} %copy.200), calls=%async_computation.1 | async-start | bytes 1900544 | tf_op jit(solution)/shard_map/all_to_all | solution.py:112
  73.5 14.2 %all-to-all-done.1 = f32[225,8,128]{2,0,1:T(8,128)S(1)} async-done(((f32[225,8,128]{2,0,1:T(8,128)}), f32[225,8,128]{2,0,1:T(8,128)S(1)}, u32[]{:S(2)}, u32[]{:S(2)}) %all-to-all-start.1) | async-done | bytes 921632 | tf_op jit(solution)/shard_map/all_to_all | solution.py:112
  88.9 1.4 fusion
  91.5 1.7 %copy.232 = f32[11,8,7,1024]{3,1,2,0:T(8,128)S(1)} copy(f32[11,8,7,1024]{3,2,1,0:T(8,128)S(1)} %bitcast.165) | data formatting | bytes 5046272
  93.2 2.6 %copy.208 = f32[7168,81]{1,0:T(8,128)} copy(f32[7168,81]{0,1:T(8,128)S(1)} %bitcast.167) | data formatting | bytes 4644864 | tf_op jit(solution)/shard_map/neg | solution.py:86
  95.8 40.5 %scatter_custom_fusion.1 = f32[81,897]{0,1:T(8,128)S(1)} fusion(s32[7168]{0:T(1024)S(1)} %bitcast.204, f32[7168,81]{1,0:T(8,128)} %copy.208, f32[]{:T(128)} %constant.34.clone.1), kind=kCustom, calls=%fused_computation.25 | custom fusion | flops 580608 | bytes 291140 | tf_op jit(solution)/shard_map/scatter-add | solution.py:127
  136.3 0.8 slice.354
  137.1 0.8 slice.350
  137.9 0.7 copy.209
  138.6 18.9 %reduce-scatter.5.cloned.1.call-done = f32[81,224]{0,1:T(8,128)} async-done(((f32[81,896]{0,1:T(8,128)}), f32[81,224]{0,1:T(8,128)}) %reduce-scatter.5.cloned.1.call-update) | async-done | bytes 72592 | tf_op jit(solution)/shard_map/reduce_scatter | solution.py:129
  157.5 1.6 copy.210
  (105 shorter events, 6.1 us)
Async XLA Ops:
  7.2 0.8 copy-start
  7.2 5.3 %copy-start.5 = (s32[1024]{0:T(1024)S(1)}, s32[1024]{0:T(1024)}, u32[]{:S(2)}) copy-start(s32[1024]{0:T(1024)} %param.11) | copy-start | bytes 12292
  7.2 5.4 %copy-start.6 = (f32[2,1024]{1,0:T(2,128)S(1)}, f32[2,1024]{1,0:T(2,128)}, u32[]{:S(2)}) copy-start(f32[2,1024]{1,0:T(2,128)} %param.10) | copy-start | bytes 24580
  7.2 5.4 %copy-start.3 = (f32[6,1024]{1,0:T(8,128)S(1)}, f32[6,1024]{1,0:T(8,128)}, u32[]{:S(2)}) copy-start(f32[6,1024]{1,0:T(8,128)} %param.9) | copy-start | bytes 73732
  7.2 5.4 %copy-start.2 = (f32[18,1024]{1,0:T(8,128)S(1)}, f32[18,1024]{1,0:T(8,128)}, u32[]{:S(2)}) copy-start(f32[18,1024]{1,0:T(8,128)} %param.8) | copy-start | bytes 221188
  12.5 9.2 %copy-start.1 = (s32[7,1024]{1,0:T(8,128)S(1)}, s32[7,1024]{1,0:T(8,128)}, u32[]{:S(2)}) copy-start(s32[7,1024]{1,0:T(8,128)} %param.14) | copy-start | bytes 86020
  12.5 9.3 %copy-start.7 = (s32[1024]{0:T(1024)S(1)}, s32[1024]{0:T(1024)}, u32[]{:S(2)}) copy-start(s32[1024]{0:T(1024)} %param.13) | copy-start | bytes 12292
  12.5 9.4 %copy-start.4 = (s32[7,1024]{1,0:T(8,128)S(1)}, s32[7,1024]{1,0:T(8,128)}, u32[]{:S(2)}) copy-start(s32[7,1024]{1,0:T(8,128)} %param.15) | copy-start | bytes 86020
  16.6 10.7 %all-to-all-start = ((f32[26,8,128]{2,0,1:T(8,128)}), f32[26,8,128]{2,0,1:T(8,128)S(1)}, u32[]{:S(2)}, u32[]{:S(2)}) async-start(f32[26,8,128]{2,0,1:T(8,128)} %copy_select_fusion), calls=%async_computation | async-start | bytes 262144 | tf_op jit(solution)/shard_map/all_to_all | solution.py:98
  69.8 17.8 %all-to-all-start.1 = ((f32[225,8,128]{2,0,1:T(8,128)}), f32[225,8,128]{2,0,1:T(8,128)S(1)}, u32[]{:S(2)}, u32[]{:S(2)}) async-start(f32[225,8,128]{2,0,1:T(8,128)} %copy.200), calls=%async_computation.1 | async-start | bytes 1900544 | tf_op jit(solution)/shard_map/all_to_all | solution.py:112
  73.4 63.7 %reduce-scatter.3.cloned.1.call-start = ((), (), s32[]{:S(2)}) async-start(), calls=%async_computation.4 | async-start | bytes 40960 | tf_op jit(solution)/shard_map/reduce_scatter | solution.py:125
  90.3 67.2 %reduce-scatter.5.cloned.1.call-start = ((), (), s32[]{:S(2)}) async-start(), calls=%async_computation.5 | async-start | bytes 573440 | tf_op jit(solution)/shard_map/reduce_scatter | solution.py:129
Sparse Core Ops, SparseCore 0:
  90.5 18.3 reduce-scatter.2
  137.2 20.2 reduce-scatter.4
where the time goes:
time: 167 us; the launch traced here: 166 us
  local copies, waits for them, and re-layouts  53.7 us (32%)
  other arithmetic  49.2 us (29%)
  waiting for transfers between devices  37.9 us (23%)
  between operations  14.8 us (9%)
  starting transfers between devices  8.99 us (5%)
    scatter-add x1, other arithmetic, on_device(): jnp.zeros((81, slot_count + 1), jnp.float32).at[:, pair_slot.reshape(-1)]  40.5 us
    gather x3, local copies, waits for them, and re-layouts, on_device(): chosen = jnp.take(flat_factor, partner.reshape(-1), axis=1)  26.9 us
    reduce_scatter x1, waiting for transfers between devices, on_device(): lax.psum_scatter(pair_total[:, :slot_count], 'row', scatter_dimension=1,...  18.9 us
    all_to_all x1, waiting for transfers between devices, on_device(): lax.all_to_all(together, 'obs', split_axis=1, concat_axis=1, tiled=True)  14.2 us
    scatter-add x1, other arithmetic, eliminate(): jnp.zeros((9, track_count), jnp.float32).at[:, track_of].add(normal)  6.09 us
    unnamed x47, local copies, waits for them, and re-layouts  5.8 us
    all_to_all x1, starting transfers between devices, on_device(): owned = lax.all_to_all(sent, 'obs', split_axis=1, concat_axis=1, tiled=True)  5.17 us
    all_to_all x1, waiting for transfers between devices, on_device(): owned = lax.all_to_all(sent, 'obs', split_axis=1, concat_axis=1, tiled=True)  4.81 us
  transfers between devices with their start and end apart: 4, of which 3 were waited for; matrix products, arithmetic and copies ran while one was open for 29% of the time, Pallas kernels for 0%

commit v1 on v0

--- a/solution.py
+++ b/solution.py
@@ -1,10 +1,384 @@
+import functools
+
 import jax
 import jax.numpy as jnp
 from jax import lax
+from jax.experimental import pallas as pl
+from jax.experimental.pallas import tpu as pltpu
 from jax.sharding import PartitionSpec as P
 
 CAM_ROW = 16
 NBR = 14
+LANES = 128
+SUBLANES = 8
+CHUNK = 256
+VMEM_BYTES = 48 * 1024 * 1024
+
+
+def lane_gather(values, index):
+    return jnp.take_along_axis(values, index, axis=1, mode="promise_in_bounds")
+
+
+def permute_kernel(camera_ref, point_ref, resid_ref, order_ref, ids_ref, sent_ref, cam_ref):
+    blocks = order_ref.shape[0]
+    order = order_ref[...]
+    block_of = lax.shift_right_logical(order, LANES.bit_length() - 1)
+    lane_of = lax.bitwise_and(order, LANES - 1)
+
+    def permuted(row_of_block):
+        total = None
+        for b in range(blocks):
+            row = jnp.broadcast_to(row_of_block(b), (blocks, LANES))
+            picked = lane_gather(row, lane_of)
+            total = picked if b == 0 else jnp.where(block_of == b, picked, total)
+        return total
+
+    start = 0
+    for ref in (camera_ref, point_ref, resid_ref):
+        for f in range(ref.shape[0]):
+            sent_ref[start + f] = permuted(
+                lambda b: ref[f : f + 1, b * LANES : (b + 1) * LANES]
+            )
+        start += ref.shape[0]
+    cam_ref[...] = permuted(lambda b: ids_ref[b : b + 1, :])
+
+
+def exchange_kernel(
+    n, sent_ref, partner_ref, recv_ref, part_ref, staged, send_sem, recv_sem, id_send, id_recv
+):
+    me = lax.axis_index("obs")
+    ranks = partner_ref.shape[0]
+    barrier = pltpu.get_barrier_semaphore()
+    for d in range(1, n):
+        pl.semaphore_signal(
+            barrier,
+            inc=1,
+            device_id={"obs": lax.rem(me + d, n)},
+            device_id_type=pl.DeviceIdType.MESH,
+        )
+    for x in range(n):
+        staged[x] = jnp.zeros((SUBLANES, LANES), jnp.int32)
+        staged[x, 0:ranks] = partner_ref[:, x * LANES : (x + 1) * LANES]
+    pl.semaphore_wait(barrier, n - 1)
+
+    def rows_copy(d):
+        peer = lax.rem(me + d, n)
+        return pltpu.make_async_remote_copy(
+            src_ref=sent_ref,
+            dst_ref=recv_ref.at[me],
+            send_sem=send_sem.at[peer],
+            recv_sem=recv_sem.at[me],
+            device_id={"obs": peer},
+            device_id_type=pl.DeviceIdType.MESH,
+        )
+
+    def ids_copy(d):
+        peer = lax.rem(me + d, n)
+        return pltpu.make_async_remote_copy(
+            src_ref=staged.at[peer],
+            dst_ref=part_ref.at[me],
+            send_sem=id_send.at[peer],
+            recv_sem=id_recv.at[me],
+            device_id={"obs": peer},
+            device_id_type=pl.DeviceIdType.MESH,
+        )
+
+    for d in range(1, n):
+        ids_copy(d).start()
+        rows_copy(d).start()
+    part_ref[me] = staged[me]
+    for d in range(1, n):
+        peer = lax.rem(me + n - d, n)
+        pltpu.make_async_remote_copy(
+            src_ref=staged.at[peer],
+            dst_ref=part_ref.at[peer],
+            send_sem=id_send.at[peer],
+            recv_sem=id_recv.at[peer],
+            device_id={"obs": peer},
+            device_id_type=pl.DeviceIdType.MESH,
+        ).wait_recv()
+        pltpu.make_async_remote_copy(
+            src_ref=sent_ref,
+            dst_ref=recv_ref.at[peer],
+            send_sem=send_sem.at[peer],
+            recv_sem=recv_sem.at[peer],
+            device_id={"obs": peer},
+            device_id_type=pl.DeviceIdType.MESH,
+        ).wait_recv()
+    for d in range(1, n):
+        ids_copy(d).wait_send()
+        rows_copy(d).wait_send()
+
+
+def normal_rows(camera_point):
+    a, b, e = camera_point[0:3], camera_point[3:6], camera_point[6:8]
+    return [
+        a[0] * a[0] + b[0] * b[0],
+        a[0] * a[1] + b[0] * b[1],
+        a[0] * a[2] + b[0] * b[2],
+        a[1] * a[1] + b[1] * b[1],
+        a[1] * a[2] + b[1] * b[2],
+        a[2] * a[2] + b[2] * b[2],
+        a[0] * e[0] + b[0] * e[1],
+        a[1] * e[0] + b[1] * e[1],
+        a[2] * e[0] + b[2] * e[1],
+    ]
+
+
+def terms_kernel(
+    n, cameras, sent_ref, cam_ref, recv_ref, part_ref, pair_ref, out_ref,
+    pairs, rows_of, offset_of, solve, own, factor_of, prod, marks,
+):
+    ranks = pair_ref.shape[0]
+    shift = LANES.bit_length() - 1
+    cam = cam_ref[...]
+    for j in range(n):
+        pairs[pl.ds(j, ranks, stride=n), :] = pair_ref[:, j * LANES : (j + 1) * LANES]
+    sources, places, offsets = [], [], []
+    for k in range(ranks):
+        slot = part_ref[pl.ds(k, n, stride=SUBLANES), :]
+        pair = pairs[pl.ds(k * n, n), :]
+        sources.append(
+            jnp.where(pair == cameras * NBR, -1, lax.shift_right_logical(slot, shift))
+        )
+        places.append(lax.bitwise_and(slot, LANES - 1))
+        offsets.append(pair - cam * NBR)
+
+    def add_source(x, totals):
+        place = jnp.zeros((n, LANES), jnp.int32)
+        offset = jnp.full((n, LANES), -1, jnp.int32)
+        for k in range(ranks):
+            match = sources[k] == x
+            place = jnp.where(match, places[k], place)
+            offset = jnp.where(match, offsets[k], offset)
+        offset_of[x] = offset
+        found = offset >= 0
+        values = []
+        for f in range(26):
+            value = jnp.where(found, lane_gather(recv_ref[x, f], place), 0.0)
+            values.append(value)
+            if f < 24:
+                rows_of[x, f] = value
+        return tuple(t + v for t, v in zip(totals, normal_rows(values[18:26])))
+
+    totals = normal_rows([sent_ref[f] for f in range(18, 26)])
+    totals = lax.fori_loop(0, n, add_source, tuple(totals))
+    pivot_one = jnp.sqrt(totals[0] + 1.0)
+    inv_one = 1.0 / pivot_one
+    low_one = totals[1] * inv_one
+    low_two = totals[2] * inv_one
+    inv_two = 1.0 / jnp.sqrt(totals[3] + 1.0 - low_one * low_one)
+    low_mid = (totals[4] - low_two * low_one) * inv_two
+    inv_three = 1.0 / jnp.sqrt(totals[5] + 1.0 - low_two * low_two - low_mid * low_mid)
+    h_one = totals[6] * inv_one
+    h_two = (totals[7] - low_one * h_one) * inv_two
+    h_three = (totals[8] - low_two * h_one - low_mid * h_two) * inv_three
+    for i, value in enumerate([inv_one, low_one, low_two, inv_two, low_mid, inv_three]):
+        solve[i] = value
+
+    def factors(rows):
+        tri = [solve[i] for i in range(6)]
+        columns = []
+        for i in range(2):
+            jp = [rows(18 + 3 * i + c) for c in range(3)]
+            one = jp[0] * tri[0]
+            two = (jp[1] - tri[1] * one) * tri[3]
+            three = (jp[2] - tri[2] * one - tri[4] * two) * tri[5]
+            columns.append((one, two, three))
+        result = [[None] * 9 for _ in range(3)]
+        for p in range(9):
+            first, second = rows(p), rows(9 + p)
+            for c in range(3):
+                result[c][p] = first * columns[0][c] + second * columns[1][c]
+        return result
+
+    mine = factors(lambda f: sent_ref[f])
+    jac = [sent_ref[f] for f in range(18)]
+    for c in range(3):
+        for p in range(9):
+            own[c * 9 + p] = -mine[c][p]
+    base = NBR * 81
+
+    def put(row, value):
+        prod[pl.ds(row * n, n), :] = value
+
+    for p in range(9):
+        for q in range(p, 9):
+            value = jac[p] * jac[q] + jac[9 + p] * jac[9 + q]
+            value = value - (
+                mine[0][p] * mine[0][q] + mine[1][p] * mine[1][q] + mine[2][p] * mine[2][q]
+            )
+            put(base + 9 * p + q, value)
+            if q != p:
+                put(base + 9 * q + p, value)
+        back = mine[0][p] * h_one + mine[1][p] * h_two + mine[2][p] * h_three
+        put(base + 81 + p, jac[p] * sent_ref[24] + jac[9 + p] * sent_ref[25] - back)
+
+    def source_factors(x, carry):
+        got = factors(lambda f: rows_of[x, f])
+        for c in range(3):
+            for p in range(9):
+                factor_of[x, c * 9 + p] = got[c][p]
+        return carry
+
+    lax.fori_loop(0, n, source_factors, 0)
+
+    def at_offset(o, carry):
+        picked = [None] * 27
+        for x in range(n):
+            match = offset_of[x] == o
+            for i in range(27):
+                value = jnp.where(match, factor_of[x, i], 0.0)
+                picked[i] = value if x == 0 else picked[i] + value
+        for p in range(9):
+            left = [own[c * 9 + p] for c in range(3)]
+            for q in range(9):
+                value = left[0] * picked[q] + left[1] * picked[9 + q] + left[2] * picked[18 + q]
+                prod[pl.ds((o * 81 + 9 * p + q) * n, n), :] = value
+        return carry
+
+    lax.fori_loop(0, NBR, at_offset, 0)
+
+    ids = lax.broadcasted_iota(jnp.int32, (cameras, LANES), 0)
+    halves = [
+        jnp.where(ids == cam[j : j + 1, :], 1.0, 0.0).astype(jnp.bfloat16) for j in range(n)
+    ]
+    for i in range(n // 2):
+        marks[i] = jnp.concatenate([halves[2 * i], halves[2 * i + 1]], axis=1)
+    contract = (((1,), (1,)), ((), ()))
+    chunks = out_ref.shape[1] // CHUNK
+
+    for ch in range(chunks):
+        total = jnp.zeros((cameras, CHUNK), jnp.float32)
+        for i in range(n // 2):
+            first = prod[pl.ds(ch * CHUNK * n + 2 * i, CHUNK, stride=n), :]
+            second = prod[pl.ds(ch * CHUNK * n + 2 * i + 1, CHUNK, stride=n), :]
+            both = jnp.concatenate([first, second], axis=1)
+            high = both.astype(jnp.bfloat16)
+            low = (both - high.astype(jnp.float32)).astype(jnp.bfloat16)
+            for half in (high, low):
+                total += lax.dot_general(
+                    marks[i], half, contract, preferred_element_type=jnp.float32
+                )
+        out_ref[:, ch * CHUNK : (ch + 1) * CHUNK] = total
+
+
+def sum_kernel(n, part_ref, out_ref, landed, send_sem, recv_sem):
+    me = lax.axis_index("row")
+    rows = out_ref.shape[0]
+    barrier = pltpu.get_barrier_semaphore()
+    for d in range(1, n):
+        pl.semaphore_signal(
+            barrier,
+            inc=1,
+            device_id={"row": lax.rem(me + d, n)},
+            device_id_type=pl.DeviceIdType.MESH,
+        )
+    pl.semaphore_wait(barrier, n - 1)
+
+    def block(peer):
+        return part_ref.at[pl.ds(pl.multiple_of(peer * rows, SUBLANES), rows)]
+
+    def copy(peer, slot):
+        return pltpu.make_async_remote_copy(
+            src_ref=block(peer),
+            dst_ref=landed.at[slot],
+            send_sem=send_sem.at[peer],
+            recv_sem=recv_sem.at[slot],
+            device_id={"row": peer},
+            device_id_type=pl.DeviceIdType.MESH,
+        )
+
+    for d in range(1, n):
+        copy(lax.rem(me + d, n), me).start()
+    total = part_ref[pl.ds(pl.multiple_of(me * rows, SUBLANES), rows), :]
+    for d in range(1, n):
+        peer = lax.rem(me + d, n)
+        copy(peer, peer).wait_recv()
+        total = total + landed[peer]
+    out_ref[...] = total
+    for d in range(1, n):
+        copy(lax.rem(me + d, n), me).wait_send()
+
+
+def by_lanes(
+    camera_jacobian, point_jacobian, residual, send_order, camera_of, track_of, partner, pair_slot
+):
+    n = lax.axis_size("obs")
+    n_row = lax.axis_size("row")
+    cameras = CAM_ROW * n_row
+    ranks = partner.shape[0]
+    width = -(-(NBR * 81 + 90) // CHUNK) * CHUNK
+    vmem = pl.BlockSpec(memory_space=pltpu.VMEM)
+    f32, i32 = jnp.float32, jnp.int32
+    sent, cam = pl.pallas_call(
+        permute_kernel,
+        out_shape=(
+            jax.ShapeDtypeStruct((26, n, LANES), f32),
+            jax.ShapeDtypeStruct((n, LANES), i32),
+        ),
+        in_specs=[vmem] * 5,
+        out_specs=(vmem, vmem),
+        name="permute",
+    )(
+        camera_jacobian,
+        point_jacobian,
+        residual,
+        send_order.reshape(n, LANES),
+        camera_of.reshape(n, LANES),
+    )
+    recv, part = pl.pallas_call(
+        functools.partial(exchange_kernel, n),
+        out_shape=(
+            jax.ShapeDtypeStruct((n, 26, n, LANES), f32),
+            jax.ShapeDtypeStruct((n, SUBLANES, LANES), i32),
+        ),
+        in_specs=[vmem] * 2,
+        out_specs=(vmem, vmem),
+        scratch_shapes=[
+            pltpu.VMEM((n, SUBLANES, LANES), i32),
+            pltpu.SemaphoreType.DMA((n,)),
+            pltpu.SemaphoreType.DMA((n,)),
+            pltpu.SemaphoreType.DMA((n,)),
+            pltpu.SemaphoreType.DMA((n,)),
+        ],
+        compiler_params=pltpu.CompilerParams(collective_id=0, has_side_effects=True),
+        name="exchange",
+    )(sent, partner)
+    partial = pl.pallas_call(
+        functools.partial(terms_kernel, n, cameras),
+        out_shape=jax.ShapeDtypeStruct((cameras, width), f32),
+        in_specs=[vmem] * 5,
+        out_specs=vmem,
+        scratch_shapes=[
+            pltpu.VMEM((ranks * n, LANES), i32),
+            pltpu.VMEM((n, 24, n, LANES), f32),
+            pltpu.VMEM((n, n, LANES), i32),
+            pltpu.VMEM((6, n, LANES), f32),
+            pltpu.VMEM((27, n, LANES), f32),
+            pltpu.VMEM((n, 27, n, LANES), f32),
+            pltpu.VMEM((width * n, LANES), f32),
+            pltpu.VMEM((n // 2, cameras, 2 * LANES), jnp.bfloat16),
+        ],
+        compiler_params=pltpu.CompilerParams(vmem_limit_bytes=VMEM_BYTES),
+        name="terms",
+    )(sent, cam, recv, part.reshape(n * SUBLANES, LANES), pair_slot)
+    mine = pl.pallas_call(
+        functools.partial(sum_kernel, n_row),
+        out_shape=jax.ShapeDtypeStruct((CAM_ROW, width), f32),
+        in_specs=[vmem],
+        out_specs=vmem,
+        scratch_shapes=[
+            pltpu.VMEM((n_row, CAM_ROW, width), f32),
+            pltpu.SemaphoreType.DMA((n_row,)),
+            pltpu.SemaphoreType.DMA((n_row,)),
+        ],
+        compiler_params=pltpu.CompilerParams(collective_id=1, has_side_effects=True),
+        name="row_sum",
+    )(partial)
+    base = NBR * 81
+    pair = mine[:, :base].reshape(CAM_ROW, NBR, 81).transpose(2, 0, 1).reshape(81, CAM_ROW * NBR)
+    return (mine[:, base : base + 81].T, mine[:, base + 81 : base + 90].T, pair)
 
 
 damping = 1.0
@@ -130,9 +504,16 @@
     return (camera_mine[:81], camera_mine[81:], pair_mine)
 
 
+def on_mesh(*arguments):
+    share = arguments[0].shape[1] // lax.axis_size("obs")
+    if share == LANES and lax.axis_size("obs") % 2 == 0:
+        return by_lanes(*arguments)
+    return on_device(*arguments)
+
+
 def solution(mesh):
     return jax.shard_map(
-        on_device,
+        on_mesh,
         mesh=mesh,
         in_specs=(
             P(None, ("obs", "row")),

time: 167 us -> 44 us (0.26)
  other arithmetic: 49.2 us -> 0 us
  local copies, waits for them, and re-layouts: 53.7 us -> 7.89 us
  waiting for transfers between devices: 37.9 us -> 0 us
  Pallas kernels: 0 us -> 34.9 us
  between operations: 14.8 us -> 0.71 us
  starting transfers between devices: 8.99 us -> 0 us
    scatter-add x2 -> x0, other arithmetic: 46.6 us -> none  [the longest x1 40.5 us: on_device(): jnp.zeros((81, slot_count + 1), jnp.float32).at[:, pair_slot.reshape(-1)]]
    gather x8 -> x0, local copies, waits for them, and re-layouts: 37.3 us -> none  [the longest x3 26.9 us: on_device(): chosen = jnp.take(flat_factor, partner.reshape(-1), axis=1)]
    pallas_call x0 -> x4, Pallas kernels: none -> 34.9 us  [the longest x1 16.1 us: by_lanes(): pl.pallas_call(functools.partial(exchange_kernel, n), out_shape=(jax.Shap...]
    all_to_all x2 -> x0, waiting for transfers between devices: 19 us -> none  [the longest x1 14.2 us: on_device(): lax.all_to_all(together, 'obs', split_axis=1, concat_axis=1, tiled=True)]
    reduce_scatter x2 -> x0, waiting for transfers between devices: 18.9 us -> none  [the longest x1 18.9 us: on_device(): lax.psum_scatter(pair_total[:, :slot_count], 'row', scatter_dimension=1,...]
    all_to_all x2 -> x0, starting transfers between devices: 8.72 us -> none  [the longest x1 5.17 us: on_device(): owned = lax.all_to_all(sent, 'obs', split_axis=1, concat_axis=1, tiled=True)]
    slice x20 -> x2, local copies, waits for them, and re-layouts: 5.28 us -> 0.88 us  [by_lanes(): mine[:, :base].reshape(CAM_ROW, NBR, 81).transpose(2, 0, 1)]
    neg x1 -> x0, local copies, waits for them, and re-layouts: 2.59 us -> none  [pair_product(): return -total.reshape(81, -1)]
  transfers between devices with their start and end apart: 4 -> 0, of which waited for: 3 -> 0; matrix products, arithmetic and copies ran while one was open for 29% -> 0% of each run, Pallas kernels for 0% -> 0%
where the time goes in v1:
time: 44 us; the launch traced here: 43.5 us
  Pallas kernels  34.9 us (79%)
  local copies, waits for them, and re-layouts  7.89 us (18%)
  between operations  0.71 us (2%)
    pallas_call x1, Pallas kernels, by_lanes(): pl.pallas_call(functools.partial(exchange_kernel, n), out_shape=(jax.Shap...  16.1 us
    pallas_call x1, Pallas kernels, by_lanes(): pl.pallas_call(functools.partial(sum_kernel, n_row), out_shape=jax.ShapeD...  12.5 us
    unnamed x14, local copies, waits for them, and re-layouts  4.71 us
    pallas_call x1, Pallas kernels, by_lanes(): pl.pallas_call(functools.partial(terms_kernel, n, cameras), out_shape=jax...  4.44 us
    transpose x2, local copies, waits for them, and re-layouts, by_lanes(): return (mine[:, base:base + 81].T, mine[:, base + 81:base + 90].T, pair)  2.16 us
    pallas_call x1, Pallas kernels, by_lanes(): pl.pallas_call(permute_kernel, out_shape=(jax.ShapeDtypeStruct((26, n, LA...  1.89 us
    slice x2, local copies, waits for them, and re-layouts, by_lanes(): mine[:, :base].reshape(CAM_ROW, NBR, 81).transpose(2, 0, 1)  0.88 us

profile of v1, /device:TPU:0, one launch (start us, length us, event | category | flops | bytes accessed | tf_op | source)
XLA Modules:
  0.0 43.5 jit_solution(6804955134494768627)
XLA Ops:
  0.6 1.9 %permute.1 = (f32[26,8,128]{2,1,0:T(8,128)}, s32[8,128]{1,0:T(8,128)}) custom-call(f32[18,1024]{1,0:T(8,128)} %camera_ref.1, f32[6,1024]{1,0:T(8,128)} %point_ref.1, f32[2,1024]{1,0:T(2,128)} %resid_ref.1, s32[8,128]{1,0:T(8,128)} %bitcast.12, s32[8,128]{1,0:T(8,128)} %bitcast.13), custom_call_target="tpu_custom_call" | custom-call | tf_op jit(solution)/shard_map/permute/pallas_call | solution.py:314
  2.5 0.0 copy-start.2
  2.5 0.0 copy-start.3
  2.5 16.1 %exchange.1 = (f32[8,26,8,128]{3,2,1,0:T(8,128)}, s32[8,8,128]{2,1,0:T(8,128)}) custom-call(f32[26,8,128]{2,1,0:T(8,128)} %get-tuple-element.7.sent_ref, s32[7,1024]{1,0:T(8,128)} %partner_ref.1), custom_call_target="tpu_custom_call" | custom-call | tf_op jit(solution)/shard_map/exchange/pallas_call | solution.py:330
  18.7 0.0 copy-start.5
  18.7 0.0 copy-done.2
  18.7 0.0 copy-done.3
  18.7 0.7 %copy-done.5 = s32[8,128]{1,0:T(8,128)S(1)} copy-done((s32[8,128]{1,0:T(8,128)S(1)}, s32[8,128]{1,0:T(8,128)}, u32[]{:S(2)}) %copy-start.5) | copy-done | bytes 4120
  19.4 0.0 copy-start.1
  19.4 1.2 %copy-done.1 = f32[8,26,8,128]{3,2,1,0:T(8,128)S(1)} copy-done((f32[8,26,8,128]{3,2,1,0:T(8,128)S(1)}, f32[8,26,8,128]{3,2,1,0:T(8,128)}, u32[]{:S(2)}) %copy-start.1) | copy-done | bytes 851992
  20.5 0.0 copy-start.4
  20.5 0.8 %copy-done.4 = s32[8,8,128]{2,1,0:T(8,128)S(1)} copy-done((s32[8,8,128]{2,1,0:T(8,128)S(1)}, s32[8,8,128]{2,1,0:T(8,128)}, u32[]{:S(2)}) %copy-start.4) | copy-done | bytes 32792
  21.3 4.4 %terms.1.part_ref = f32[64,1280]{1,0:T(8,128)S(1)} custom-call(f32[26,8,128]{2,1,0:T(8,128)S(1)} %copy-done.2, s32[8,128]{1,0:T(8,128)S(1)} %copy-done.5, f32[8,26,8,128]{3,2,1,0:T(8,128)S(1)} %copy-done.1, s32[64,128]{1,0:T(8,128)S(1)} %bitcast.10, s32[7,1024]{1,0:T(8,128)S(1)} %copy-done.3), custom_call_target="tpu_custom_call" | custom-call | tf_op jit(solution)/shard_map/terms/pallas_call | solution.py:348
  25.7 0.0 copy-start
  25.7 0.7 %copy-done = f32[64,1280]{1,0:T(8,128)} copy-done((f32[64,1280]{1,0:T(8,128)}, f32[64,1280]{1,0:T(8,128)S(1)}, u32[]{:S(2)}) %copy-start) | copy-done | bytes 327704
  26.4 12.5 %row_sum.1 = f32[16,1280]{1,0:T(8,128)} custom-call(f32[64,1280]{1,0:T(8,128)} %copy-done), custom_call_target="tpu_custom_call" | custom-call | tf_op jit(solution)/shard_map/row_sum/pallas_call | solution.py:366
  38.9 0.8 %slice_bitcast_fusion = f32[9,16]{0,1:T(8,128)S(1)} fusion(f32[16,1280]{1,0:T(8,128)} %row_sum.1), kind=kLoop, calls=%fused_computation | loop fusion | bytes 1152 | tf_op jit(solution)/shard_map/transpose | solution.py:381
  39.7 0.7 %copy.12 = f32[9,16]{1,0:T(8,128)} copy(f32[9,16]{0,1:T(8,128)S(1)} %slice_bitcast_fusion) | data formatting | bytes 1152
  40.4 1.4 %slice_bitcast_fusion.1 = f32[81,16]{0,1:T(8,128)} fusion(f32[16,1280]{1,0:T(8,128)} %row_sum.1), kind=kLoop, calls=%fused_computation.1 | loop fusion | bytes 10368 | tf_op jit(solution)/shard_map/transpose | solution.py:381
  41.7 0.0 slice-start
  41.8 0.9 %slice-done = f32[16,1134]{1,0:T(8,128)S(1)} async-done(((f32[16,1280]{1,0:T(8,128)}), f32[16,1134]{1,0:T(8,128)S(1)}, s32[]{:S(2)}) %slice-start) | async-done | bytes 72600 | tf_op jit(solution)/shard_map/slice | solution.py:380
  42.6 0.1 reshape.24
  42.8 0.7 %copy.13 = f32[81,224]{1,0:T(8,128)} copy(f32[81,224]{0,1:T(8,128)S(1)} %reshape.25) | data formatting | bytes 145152
  (1 shorter events, 0.0 us)
Async XLA Ops:
  2.5 16.2 %copy-start.2 = (f32[26,8,128]{2,1,0:T(8,128)S(1)}, f32[26,8,128]{2,1,0:T(8,128)}, u32[]{:S(2)}) copy-start(f32[26,8,128]{2,1,0:T(8,128)} %get-tuple-element.7.sent_ref) | copy-start | bytes 319492
  2.5 16.2 %copy-start.3 = (s32[7,1024]{1,0:T(8,128)S(1)}, s32[7,1024]{1,0:T(8,128)}, u32[]{:S(2)}) copy-start(s32[7,1024]{1,0:T(8,128)} %pair_ref.1) | copy-start | bytes 86020
  18.7 0.7 %copy-start.5 = (s32[8,128]{1,0:T(8,128)S(1)}, s32[8,128]{1,0:T(8,128)}, u32[]{:S(2)}) copy-start(s32[8,128]{1,0:T(8,128)} %get-tuple-element.8.cam_ref) | copy-start | bytes 12292
  19.4 1.2 %copy-start.1 = (f32[8,26,8,128]{3,2,1,0:T(8,128)S(1)}, f32[8,26,8,128]{3,2,1,0:T(8,128)}, u32[]{:S(2)}) copy-start(f32[8,26,8,128]{3,2,1,0:T(8,128)} %get-tuple-element.9.recv_ref) | copy-start | bytes 2555908
  20.5 0.8 %copy-start.4 = (s32[8,8,128]{2,1,0:T(8,128)S(1)}, s32[8,8,128]{2,1,0:T(8,128)}, u32[]{:S(2)}) copy-start(s32[8,8,128]{2,1,0:T(8,128)} %get-tuple-element.10) | copy-start | bytes 98308
  25.7 0.7 %copy-start = (f32[64,1280]{1,0:T(8,128)}, f32[64,1280]{1,0:T(8,128)S(1)}, u32[]{:S(2)}) copy-start(f32[64,1280]{1,0:T(8,128)S(1)} %terms.1.part_ref) | copy-start | bytes 983044
  41.7 0.9 %slice-start = ((f32[16,1280]{1,0:T(8,128)}), f32[16,1134]{1,0:T(8,128)S(1)}, s32[]{:S(2)}) async-start(f32[16,1280]{1,0:T(8,128)} %row_sum.1), calls=%async_computation | async-start | bytes 147456 | tf_op jit(solution)/shard_map/slice | solution.py:380

commit v2 on v0

--- a/solution.py
+++ b/solution.py
@@ -1,10 +1,396 @@
+import functools
+
 import jax
 import jax.numpy as jnp
 from jax import lax
+from jax.experimental import pallas as pl
+from jax.experimental.pallas import tpu as pltpu
 from jax.sharding import PartitionSpec as P
 
 CAM_ROW = 16
 NBR = 14
+LANES = 128
+SUBLANES = 8
+CHUNK = 256
+PACK = 3
+PIECES = 2
+MESH = pl.DeviceIdType.MESH
+VMEM_BYTES = 48 * 1024 * 1024
+
+
+def lane_gather(values, index):
+    return jnp.take_along_axis(values, index, axis=1, mode="promise_in_bounds")
+
+
+def normal_rows(camera_point):
+    a, b, e = camera_point[0:3], camera_point[3:6], camera_point[6:8]
+    return [
+        a[0] * a[0] + b[0] * b[0],
+        a[0] * a[1] + b[0] * b[1],
+        a[0] * a[2] + b[0] * b[2],
+        a[1] * a[1] + b[1] * b[1],
+        a[1] * a[2] + b[1] * b[2],
+        a[2] * a[2] + b[2] * b[2],
+        a[0] * e[0] + b[0] * e[1],
+        a[1] * e[0] + b[1] * e[1],
+        a[2] * e[0] + b[2] * e[1],
+    ]
+
+
+def step_kernel(
+    n, n_row, cameras,
+    camera_ref, point_ref, resid_ref, order_ref, ids_ref, partner_ref, pair_ref,
+    hessian_ref, gradient_ref, pair_out_ref,
+    rows_in, part, staged, pairs, rows_of, offset_of, solve, own, factor_of, prod, marks,
+    partial, landed, turned,
+    id_send, id_recv, row_send, row_recv, pass_send, sum_send, sum_recv,
+):
+    me = lax.axis_index("obs")
+    my_row = lax.axis_index("row")
+    chips = n // 2
+    chip = me // 2
+    core = lax.rem(me, 2)
+    sibling = chip * 2 + 1 - core
+    ranks = partner_ref.shape[0]
+    shift = LANES.bit_length() - 1
+    size = 26 // PIECES
+    chunks = partial.shape[0]
+
+    barrier = pltpu.get_barrier_semaphore()
+    for d in range(1, n):
+        pl.semaphore_signal(
+            barrier, inc=1, device_id={"obs": lax.rem(me + d, n)}, device_id_type=MESH
+        )
+    for d in range(1, n_row):
+        pl.semaphore_signal(
+            barrier, inc=1, device_id={"row": lax.rem(my_row + d, n_row)}, device_id_type=MESH
+        )
+
+    for x in range(n):
+        staged[x] = jnp.zeros((SUBLANES, LANES), jnp.int32)
+        staged[x, 0:ranks] = partner_ref[:, x * LANES : (x + 1) * LANES]
+
+    def ids_copy(peer, source):
+        return pltpu.make_async_remote_copy(
+            src_ref=staged.at[peer],
+            dst_ref=part.at[pl.ds(pl.multiple_of(source * SUBLANES, SUBLANES), SUBLANES)],
+            send_sem=id_send.at[peer],
+            recv_sem=id_recv.at[source],
+            device_id={"obs": peer},
+            device_id_type=MESH,
+        )
+
+    def rows_copy(source, piece, peer, sem):
+        block = rows_in.at[source, pl.ds(piece * size, size)]
+        return pltpu.make_async_remote_copy(
+            src_ref=block,
+            dst_ref=block,
+            send_sem=sem.at[peer if sem is row_send else source, piece],
+            recv_sem=row_recv.at[source, piece],
+            device_id={"obs": peer},
+            device_id_type=MESH,
+        )
+
+    def twin(d):
+        return lax.rem(chip + d, chips) * 2 + core
+
+    order = order_ref[...]
+    block_of = lax.shift_right_logical(order, shift)
+    lane_of = lax.bitwise_and(order, LANES - 1)
+
+    def permuted(row_of_block):
+        total = None
+        for b in range(n):
+            row = jnp.broadcast_to(row_of_block(b), (n, LANES))
+            picked = lane_gather(row, lane_of)
+            total = picked if b == 0 else jnp.where(block_of == b, picked, total)
+        return total
+
+    table = [(point_ref, f) for f in range(6)] + [(resid_ref, f) for f in range(2)]
+    table = table + [(camera_ref, f) for f in range(18)]
+    targets = [twin(d) for d in range(1, chips)] + [sibling]
+    for piece in range(PIECES):
+        for f in range(piece * size, (piece + 1) * size):
+            ref, r = table[f]
+            rows_in[me, f] = permuted(lambda b: ref[r : r + 1, b * LANES : (b + 1) * LANES])
+        if piece == 0:
+            pl.semaphore_wait(barrier, n - 1 + n_row - 1)
+        for peer in targets:
+            rows_copy(me, piece, peer, row_send).start()
+        if piece == 0:
+            for d in range(1, n):
+                ids_copy(lax.rem(me + d, n), me).start()
+    part[pl.ds(pl.multiple_of(me * SUBLANES, SUBLANES), SUBLANES), :] = staged[me]
+
+    cam = permuted(lambda b: ids_ref[b : b + 1, :])
+    ids = lax.broadcasted_iota(jnp.int32, (cameras, LANES), 0)
+    halves = [
+        jnp.where(ids == cam[j : j + 1, :], 1.0, 0.0).astype(jnp.bfloat16) for j in range(n)
+    ]
+    for i in range(n // 2):
+        marks[i] = jnp.concatenate([halves[2 * i], halves[2 * i + 1]], axis=1)
+    for j in range(n):
+        pairs[pl.ds(j, ranks, stride=n), :] = pair_ref[:, j * LANES : (j + 1) * LANES]
+    turned[...] = jnp.zeros_like(turned)
+    pair_out_ref[...] = jnp.zeros_like(pair_out_ref)
+
+    for d in range(1, n):
+        peer = lax.rem(me + d, n)
+        ids_copy(peer, peer).wait_recv()
+    sources, places, offsets = [], [], []
+    for k in range(ranks):
+        slot = part[pl.ds(k, n, stride=SUBLANES), :]
+        pair = pairs[pl.ds(k * n, n), :]
+        sources.append(
+            jnp.where(pair == cameras * NBR, -1, lax.shift_right_logical(slot, shift))
+        )
+        places.append(lax.bitwise_and(slot, LANES - 1))
+        offsets.append(pair - cam * NBR)
+
+    for d in range(1, chips):
+        for piece in range(PIECES):
+            rows_copy(twin(d), piece, sibling, row_send).wait_recv()
+            rows_copy(twin(d), piece, sibling, pass_send).start()
+    for piece in range(PIECES):
+        rows_copy(sibling, piece, sibling, row_send).wait_recv()
+
+    def add_source(t, totals):
+        x = lax.rem(chip + t // 2, chips) * 2 + lax.rem(core + t, 2)
+
+        @pl.when(jnp.logical_and(lax.rem(t, 2) == 1, t > 1))
+        def _():
+            for piece in range(PIECES):
+                rows_copy(x, piece, sibling, pass_send).wait_recv()
+
+        place = jnp.zeros((n, LANES), jnp.int32)
+        offset = jnp.full((n, LANES), -1, jnp.int32)
+        for k in range(ranks):
+            match = sources[k] == x
+            place = jnp.where(match, places[k], place)
+            offset = jnp.where(match, offsets[k], offset)
+        offset_of[t] = offset
+        found = offset >= 0
+        values = []
+        for f in range(26):
+            value = jnp.where(found, lane_gather(rows_in[x, f], place), 0.0)
+            rows_of[t, f] = value
+            values.append(value)
+        return tuple(t + v for t, v in zip(totals, normal_rows(values[0:8])))
+
+    totals = normal_rows([rows_in[me, f] for f in range(8)])
+    totals = lax.fori_loop(0, n, add_source, tuple(totals))
+    pivot_one = jnp.sqrt(totals[0] + 1.0)
+    inv_one = 1.0 / pivot_one
+    low_one = totals[1] * inv_one
+    low_two = totals[2] * inv_one
+    inv_two = 1.0 / jnp.sqrt(totals[3] + 1.0 - low_one * low_one)
+    low_mid = (totals[4] - low_two * low_one) * inv_two
+    inv_three = 1.0 / jnp.sqrt(totals[5] + 1.0 - low_two * low_two - low_mid * low_mid)
+    h_one = totals[6] * inv_one
+    h_two = (totals[7] - low_one * h_one) * inv_two
+    h_three = (totals[8] - low_two * h_one - low_mid * h_two) * inv_three
+    for i, value in enumerate([inv_one, low_one, low_two, inv_two, low_mid, inv_three]):
+        solve[i] = value
+
+    def factors(rows):
+        tri = [solve[i] for i in range(6)]
+        columns = []
+        for i in range(2):
+            jp = [rows(3 * i + c) for c in range(3)]
+            one = jp[0] * tri[0]
+            two = (jp[1] - tri[1] * one) * tri[3]
+            three = (jp[2] - tri[2] * one - tri[4] * two) * tri[5]
+            columns.append((one, two, three))
+        result = [[None] * 9 for _ in range(3)]
+        for p in range(9):
+            first, second = rows(8 + p), rows(17 + p)
+            for c in range(3):
+                result[c][p] = first * columns[0][c] + second * columns[1][c]
+        return result
+
+    mine = factors(lambda f: rows_in[me, f])
+    jac = [rows_in[me, 8 + f] for f in range(18)]
+    for c in range(3):
+        for p in range(9):
+            own[c * 9 + p] = -mine[c][p]
+    last = chunks - 1
+    base = last * CHUNK + (NBR - last * PACK) * 81
+
+    def put(row, value):
+        prod[pl.ds(row * n, n), :] = value
+
+    for p in range(9):
+        for q in range(p, 9):
+            value = jac[p] * jac[q] + jac[9 + p] * jac[9 + q]
+            value = value - (
+                mine[0][p] * mine[0][q] + mine[1][p] * mine[1][q] + mine[2][p] * mine[2][q]
+            )
+            put(base + 9 * p + q, value)
+            if q != p:
+                put(base + 9 * q + p, value)
+        back = mine[0][p] * h_one + mine[1][p] * h_two + mine[2][p] * h_three
+        put(base + 81 + p, jac[p] * rows_in[me, 6] + jac[9 + p] * rows_in[me, 7] - back)
+
+    def source_factors(x, carry):
+        got = factors(lambda f: rows_of[x, f])
+        for c in range(3):
+            for p in range(9):
+                factor_of[x, c * 9 + p] = got[c][p]
+        return carry
+
+    lax.fori_loop(0, n, source_factors, 0)
+
+    def at_offset(o, row):
+        picked = [None] * 27
+        for x in range(n):
+            match = offset_of[x] == o
+            for i in range(27):
+                value = jnp.where(match, factor_of[x, i], 0.0)
+                picked[i] = value if x == 0 else picked[i] + value
+        for p in range(9):
+            left = [own[c * 9 + p] for c in range(3)]
+            for q in range(9):
+                value = left[0] * picked[q] + left[1] * picked[9 + q] + left[2] * picked[18 + q]
+                prod[pl.ds(pl.multiple_of((row + 9 * p + q) * n, n), n), :] = value
+
+    contract = (((1,), (1,)), ((), ()))
+
+    def sum_copy(peer, slot, chunk):
+        return pltpu.make_async_remote_copy(
+            src_ref=partial.at[chunk, pl.ds(pl.multiple_of(peer * CAM_ROW, CAM_ROW), CAM_ROW)],
+            dst_ref=landed.at[slot, chunk],
+            send_sem=sum_send.at[peer, chunk],
+            recv_sem=sum_recv.at[slot, chunk],
+            device_id={"row": peer},
+            device_id_type=MESH,
+        )
+
+    def chunk_step(chunk, carry):
+        def offset_step(i, inner):
+            at_offset(chunk * PACK + i, chunk * CHUNK + i * 81)
+            return inner
+
+        lax.fori_loop(0, jnp.minimum(PACK, NBR - chunk * PACK), offset_step, 0)
+        total = jnp.zeros((cameras, CHUNK), jnp.float32)
+        for i in range(n // 2):
+            start = chunk * (CHUNK * n) + 2 * i
+            first = prod[pl.ds(start, CHUNK, stride=n), :]
+            second = prod[pl.ds(start + 1, CHUNK, stride=n), :]
+            both = jnp.concatenate([first, second], axis=1)
+            high = both.astype(jnp.bfloat16)
+            low = (both - high.astype(jnp.float32)).astype(jnp.bfloat16)
+            for half in (high, low):
+                total += lax.dot_general(
+                    marks[i], half, contract, preferred_element_type=jnp.float32
+                )
+        partial[chunk] = total
+        for d in range(1, n_row):
+            sum_copy(lax.rem(my_row + d, n_row), my_row, chunk).start()
+        return carry
+
+    lax.fori_loop(0, chunks, chunk_step, 0)
+
+    slots = pair_out_ref.shape[1]
+    lane = lax.broadcasted_iota(jnp.int32, (LANES, slots), 1)
+    line = lax.broadcasted_iota(jnp.int32, (LANES, slots), 0)
+    for chunk in range(chunks):
+        total = partial[chunk, pl.ds(pl.multiple_of(my_row * CAM_ROW, CAM_ROW), CAM_ROW), :]
+        for d in range(1, n_row):
+            peer = lax.rem(my_row + d, n_row)
+            sum_copy(peer, peer, chunk).wait_recv()
+            total = total + landed[peer, chunk]
+        count = min(PACK, NBR - chunk * PACK)
+        for i in range(count):
+            turned[i * CAM_ROW : (i + 1) * CAM_ROW, 0:81] = total[:, i * 81 : (i + 1) * 81]
+        if chunk == last:
+            turned[count * CAM_ROW : (count + 1) * CAM_ROW, 0:90] = total[
+                :, count * 81 : count * 81 + 90
+            ]
+        flipped = turned[...].T
+        offset = chunk * PACK + line // CAM_ROW
+        chosen = jnp.logical_and(
+            lane == lax.rem(line, CAM_ROW) * NBR + offset, line < count * CAM_ROW
+        )
+        select = jnp.where(chosen, 1.0, 0.0).astype(jnp.bfloat16)
+        rows = flipped[0:88]
+        high = rows.astype(jnp.bfloat16)
+        low = (rows - high.astype(jnp.float32)).astype(jnp.bfloat16)
+        placed = jnp.dot(high, select, preferred_element_type=jnp.float32)
+        placed = placed + jnp.dot(low, select, preferred_element_type=jnp.float32)
+        pair_out_ref[...] += placed[0:81]
+        if chunk == last:
+            mine_lanes = flipped[:, count * CAM_ROW : (count + 1) * CAM_ROW]
+            hessian_ref[...] = mine_lanes[0:81]
+            gradient_ref[...] = mine_lanes[81:90]
+
+    for d in range(1, n):
+        ids_copy(lax.rem(me + d, n), me).wait_send()
+    for piece in range(PIECES):
+        for peer in targets:
+            rows_copy(me, piece, peer, row_send).wait_send()
+        for d in range(1, chips):
+            rows_copy(twin(d), piece, sibling, pass_send).wait_send()
+    for chunk in range(chunks):
+        for d in range(1, n_row):
+            sum_copy(lax.rem(my_row + d, n_row), my_row, chunk).wait_send()
+
+
+def by_lanes(
+    camera_jacobian, point_jacobian, residual, send_order, camera_of, track_of, partner, pair_slot
+):
+    n = lax.axis_size("obs")
+    n_row = lax.axis_size("row")
+    cameras = CAM_ROW * n_row
+    ranks = partner.shape[0]
+    chunks = -(-NBR // PACK)
+    vmem = pl.BlockSpec(memory_space=pltpu.VMEM)
+    f32, i32 = jnp.float32, jnp.int32
+    dma = pltpu.SemaphoreType.DMA
+    return pl.pallas_call(
+        functools.partial(step_kernel, n, n_row, cameras),
+        out_shape=(
+            jax.ShapeDtypeStruct((81, CAM_ROW), f32),
+            jax.ShapeDtypeStruct((9, CAM_ROW), f32),
+            jax.ShapeDtypeStruct((81, CAM_ROW * NBR), f32),
+        ),
+        in_specs=[vmem] * 7,
+        out_specs=(vmem, vmem, vmem),
+        scratch_shapes=[
+            pltpu.VMEM((n, 26, n, LANES), f32),
+            pltpu.VMEM((n * SUBLANES, LANES), i32),
+            pltpu.VMEM((n, SUBLANES, LANES), i32),
+            pltpu.VMEM((ranks * n, LANES), i32),
+            pltpu.VMEM((n, 26, n, LANES), f32),
+            pltpu.VMEM((n, n, LANES), i32),
+            pltpu.VMEM((6, n, LANES), f32),
+            pltpu.VMEM((27, n, LANES), f32),
+            pltpu.VMEM((n, 27, n, LANES), f32),
+            pltpu.VMEM((chunks * CHUNK * n, LANES), f32),
+            pltpu.VMEM((n // 2, cameras, 2 * LANES), jnp.bfloat16),
+            pltpu.VMEM((chunks, cameras, CHUNK), f32),
+            pltpu.VMEM((n_row, chunks, CAM_ROW, CHUNK), f32),
+            pltpu.VMEM((LANES, LANES), f32),
+            dma((n,)),
+            dma((n,)),
+            dma((n, PIECES)),
+            dma((n, PIECES)),
+            dma((n, PIECES)),
+            dma((n_row, chunks)),
+            dma((n_row, chunks)),
+        ],
+        compiler_params=pltpu.CompilerParams(
+            collective_id=0, has_side_effects=True, vmem_limit_bytes=VMEM_BYTES
+        ),
+        name="gauss_newton_step",
+    )(
+        camera_jacobian,
+        point_jacobian,
+        residual,
+        send_order.reshape(n, LANES),
+        camera_of.reshape(n, LANES),
+        partner,
+        pair_slot,
+    )
 
 
 damping = 1.0
@@ -130,9 +516,16 @@
     return (camera_mine[:81], camera_mine[81:], pair_mine)
 
 
+def on_mesh(*arguments):
+    share = arguments[0].shape[1] // lax.axis_size("obs")
+    if share == LANES and lax.axis_size("obs") % 2 == 0:
+        return by_lanes(*arguments)
+    return on_device(*arguments)
+
+
 def solution(mesh):
     return jax.shard_map(
-        on_device,
+        on_mesh,
         mesh=mesh,
         in_specs=(
             P(None, ("obs", "row")),

time: 167 us -> 32.6 us (0.20)
  other arithmetic: 49.2 us -> 0 us
  local copies, waits for them, and re-layouts: 53.7 us -> 7.13 us
  waiting for transfers between devices: 37.9 us -> 0 us
  Pallas kernels: 0 us -> 24.4 us
  between operations: 14.8 us -> 0.66 us
  starting transfers between devices: 8.99 us -> 0 us
    scatter-add x2 -> x0, other arithmetic: 46.6 us -> none  [the longest x1 40.5 us: on_device(): jnp.zeros((81, slot_count + 1), jnp.float32).at[:, pair_slot.reshape(-1)]]
    gather x8 -> x0, local copies, waits for them, and re-layouts: 37.3 us -> none  [the longest x3 26.9 us: on_device(): chosen = jnp.take(flat_factor, partner.reshape(-1), axis=1)]
    pallas_call x0 -> x1, Pallas kernels: none -> 24.4 us  [by_lanes(): pl.pallas_call(functools.partial(step_kernel, n, n_row, cameras), out_sha...]
    all_to_all x2 -> x0, waiting for transfers between devices: 19 us -> none  [the longest x1 14.2 us: on_device(): lax.all_to_all(together, 'obs', split_axis=1, concat_axis=1, tiled=True)]
    reduce_scatter x2 -> x0, waiting for transfers between devices: 18.9 us -> none  [the longest x1 18.9 us: on_device(): lax.psum_scatter(pair_total[:, :slot_count], 'row', scatter_dimension=1,...]
    all_to_all x2 -> x0, starting transfers between devices: 8.72 us -> none  [the longest x1 5.17 us: on_device(): owned = lax.all_to_all(sent, 'obs', split_axis=1, concat_axis=1, tiled=True)]
    slice x20 -> x0, local copies, waits for them, and re-layouts: 5.28 us -> none  [the longest x1 2.39 us: eliminate(): per_obs[6]]
    neg x1 -> x0, local copies, waits for them, and re-layouts: 2.59 us -> none  [pair_product(): return -total.reshape(81, -1)]
  transfers between devices with their start and end apart: 4 -> 0, of which waited for: 3 -> 0; matrix products, arithmetic and copies ran while one was open for 29% -> 0% of each run, Pallas kernels for 0% -> 0%
where the time goes in v2:
time: 32.6 us; the launch traced here: 32.2 us
  Pallas kernels  24.4 us (75%)
  local copies, waits for them, and re-layouts  7.13 us (22%)
  between operations  0.66 us (2%)
    pallas_call x1, Pallas kernels, by_lanes(): pl.pallas_call(functools.partial(step_kernel, n, n_row, cameras), out_sha...  24.4 us
    unnamed x16, local copies, waits for them, and re-layouts  6.46 us
    pallas_call x1, local copies, waits for them, and re-layouts, by_lanes(): pl.pallas_call(functools.partial(step_kernel, n, n_row, cameras), out_sha...  0.67 us

profile of v2, /device:TPU:0, one launch (start us, length us, event | category | flops | bytes accessed | tf_op | source)
XLA Modules:
  0.0 32.2 jit_solution(2844047674105404050)
XLA Ops:
  0.6 0.0 copy-start
  0.6 0.9 %copy-done = f32[18,1024]{1,0:T(8,128)S(1)} copy-done((f32[18,1024]{1,0:T(8,128)S(1)}, f32[18,1024]{1,0:T(8,128)}, u32[]{:S(2)}) %copy-start) | copy-done | bytes 73752
  1.5 0.0 copy-start.1
  1.5 0.8 %copy-done.1 = f32[6,1024]{1,0:T(8,128)S(1)} copy-done((f32[6,1024]{1,0:T(8,128)S(1)}, f32[6,1024]{1,0:T(8,128)}, u32[]{:S(2)}) %copy-start.1) | copy-done | bytes 24600
  2.3 0.0 copy-start.2
  2.3 0.8 %copy-done.2 = s32[7,1024]{1,0:T(8,128)S(1)} copy-done((s32[7,1024]{1,0:T(8,128)S(1)}, s32[7,1024]{1,0:T(8,128)}, u32[]{:S(2)}) %copy-start.2) | copy-done | bytes 28696
  3.0 0.0 copy-start.3
  3.0 0.8 %copy-done.3 = s32[7,1024]{1,0:T(8,128)S(1)} copy-done((s32[7,1024]{1,0:T(8,128)S(1)}, s32[7,1024]{1,0:T(8,128)}, u32[]{:S(2)}) %copy-start.3) | copy-done | bytes 28696
  3.8 0.0 copy-start.4
  3.8 0.7 %copy-done.4 = f32[2,1024]{1,0:T(2,128)S(1)} copy-done((f32[2,1024]{1,0:T(2,128)S(1)}, f32[2,1024]{1,0:T(2,128)}, u32[]{:S(2)}) %copy-start.4) | copy-done | bytes 8216
  4.5 0.0 copy-start.5
  4.5 0.7 %copy-done.5 = s32[1024]{0:T(1024)S(1)} copy-done((s32[1024]{0:T(1024)S(1)}, s32[1024]{0:T(1024)}, u32[]{:S(2)}) %copy-start.5) | copy-done | bytes 4120
  5.2 0.0 copy-start.6
  5.2 0.7 %copy-done.6 = s32[1024]{0:T(1024)S(1)} copy-done((s32[1024]{0:T(1024)S(1)}, s32[1024]{0:T(1024)}, u32[]{:S(2)}) %copy-start.6) | copy-done | bytes 4120
  5.9 24.4 %gauss_newton_step.1 = (f32[81,16]{1,0:T(8,128)S(1)}, f32[9,16]{1,0:T(8,128)S(1)}, f32[81,224]{1,0:T(8,128)S(1)}) custom-call(f32[18,1024]{1,0:T(8,128)S(1)} %copy-done, f32[6,1024]{1,0:T(8,128)S(1)} %copy-done.1, f32[2,1024]{1,0:T(2,128)S(1)} %copy-done.4, s32[8,128]{1,0:T(8,128)S(1)} %bitcast.2, s32[8,128]{1,0:T(8,128)S(1)} %bitcast.3, ...), custom_call_target="tpu_custom_call" | custom-call | tf_op jit(solution)/shard_map/gauss_newton_step/pallas_call | solution.py:349
  30.3 0.7 %copy.10 = f32[81,16]{0,1:T(8,128)} copy(f32[81,16]{1,0:T(8,128)S(1)} %get-tuple-element.3) | data formatting | bytes 10368 | tf_op jit(solution)/shard_map/gauss_newton_step/pallas_call | solution.py:349
  30.9 0.6 %copy.13 = f32[9,16]{1,0:T(8,128)} copy(f32[9,16]{1,0:T(8,128)S(1)} %get-tuple-element.10) | data formatting | bytes 1152
  31.5 0.6 %copy.14 = f32[81,224]{1,0:T(8,128)} copy(f32[81,224]{1,0:T(8,128)S(1)} %get-tuple-element.11) | data formatting | bytes 145152
Async XLA Ops:
  0.6 0.9 %copy-start = (f32[18,1024]{1,0:T(8,128)S(1)}, f32[18,1024]{1,0:T(8,128)}, u32[]{:S(2)}) copy-start(f32[18,1024]{1,0:T(8,128)} %camera_ref.1) | copy-start | bytes 221188
  1.5 0.8 %copy-start.1 = (f32[6,1024]{1,0:T(8,128)S(1)}, f32[6,1024]{1,0:T(8,128)}, u32[]{:S(2)}) copy-start(f32[6,1024]{1,0:T(8,128)} %point_ref.1) | copy-start | bytes 73732
  2.3 0.8 %copy-start.2 = (s32[7,1024]{1,0:T(8,128)S(1)}, s32[7,1024]{1,0:T(8,128)}, u32[]{:S(2)}) copy-start(s32[7,1024]{1,0:T(8,128)} %partner_ref.1) | copy-start | bytes 86020
  3.0 0.8 %copy-start.3 = (s32[7,1024]{1,0:T(8,128)S(1)}, s32[7,1024]{1,0:T(8,128)}, u32[]{:S(2)}) copy-start(s32[7,1024]{1,0:T(8,128)} %pair_ref.1) | copy-start | bytes 86020
  3.8 0.7 %copy-start.4 = (f32[2,1024]{1,0:T(2,128)S(1)}, f32[2,1024]{1,0:T(2,128)}, u32[]{:S(2)}) copy-start(f32[2,1024]{1,0:T(2,128)} %resid_ref.1) | copy-start | bytes 24580
  4.5 0.7 %copy-start.5 = (s32[1024]{0:T(1024)S(1)}, s32[1024]{0:T(1024)}, u32[]{:S(2)}) copy-start(s32[1024]{0:T(1024)} %param.11) | copy-start | bytes 12292
  5.2 0.7 %copy-start.6 = (s32[1024]{0:T(1024)S(1)}, s32[1024]{0:T(1024)}, u32[]{:S(2)}) copy-start(s32[1024]{0:T(1024)} %param.12) | copy-start | bytes 12292

commit v3 on v2

--- a/solution.py
+++ b/solution.py
@@ -15,7 +15,7 @@
 PACK = 3
 PIECES = 2
 MESH = pl.DeviceIdType.MESH
-VMEM_BYTES = 48 * 1024 * 1024
+VMEM_BYTES = 64 * 1024 * 1024
 
 
 def lane_gather(values, index):
@@ -39,8 +39,9 @@
 
 def step_kernel(
     n, n_row, cameras,
-    camera_ref, point_ref, resid_ref, order_ref, ids_ref, partner_ref, pair_ref,
+    camera_in, point_in, resid_in, order_in, ids_in, partner_in, pair_in,
     hessian_ref, gradient_ref, pair_out_ref,
+    camera_ref, point_ref, resid_ref, order_ref, ids_ref, partner_ref, pair_ref, load_sem,
     rows_in, part, staged, pairs, rows_of, offset_of, solve, own, factor_of, prod, marks,
     partial, landed, turned,
     id_send, id_recv, row_send, row_recv, pass_send, sum_send, sum_recv,
@@ -56,6 +57,22 @@
     size = 26 // PIECES
     chunks = partial.shape[0]
 
+    moves = [
+        pltpu.make_async_copy(source, target, load_sem.at[i])
+        for i, (source, target) in enumerate(
+            [
+                (order_in, order_ref),
+                (point_in, point_ref),
+                (resid_in, resid_ref),
+                (camera_in, camera_ref),
+                (partner_in, partner_ref),
+                (ids_in, ids_ref),
+                (pair_in, pair_ref),
+            ]
+        )
+    ]
+    for move in moves:
+        move.start()
     barrier = pltpu.get_barrier_semaphore()
     for d in range(1, n):
         pl.semaphore_signal(
@@ -65,10 +82,6 @@
         pl.semaphore_signal(
             barrier, inc=1, device_id={"row": lax.rem(my_row + d, n_row)}, device_id_type=MESH
         )
-
-    for x in range(n):
-        staged[x] = jnp.zeros((SUBLANES, LANES), jnp.int32)
-        staged[x, 0:ranks] = partner_ref[:, x * LANES : (x + 1) * LANES]
 
     def ids_copy(peer, source):
         return pltpu.make_async_remote_copy(
@@ -94,6 +107,8 @@
     def twin(d):
         return lax.rem(chip + d, chips) * 2 + core
 
+    for move in moves[:4]:
+        move.wait()
     order = order_ref[...]
     block_of = lax.shift_right_logical(order, shift)
     lane_of = lax.bitwise_and(order, LANES - 1)
@@ -118,6 +133,11 @@
         for peer in targets:
             rows_copy(me, piece, peer, row_send).start()
         if piece == 0:
+            for move in moves[4:]:
+                move.wait()
+            for x in range(n):
+                staged[x] = jnp.zeros((SUBLANES, LANES), jnp.int32)
+                staged[x, 0:ranks] = partner_ref[:, x * LANES : (x + 1) * LANES]
             for d in range(1, n):
                 ids_copy(lax.rem(me + d, n), me).start()
     part[pl.ds(pl.multiple_of(me * SUBLANES, SUBLANES), SUBLANES), :] = staged[me]
@@ -147,38 +167,40 @@
         places.append(lax.bitwise_and(slot, LANES - 1))
         offsets.append(pair - cam * NBR)
 
-    for d in range(1, chips):
-        for piece in range(PIECES):
-            rows_copy(twin(d), piece, sibling, row_send).wait_recv()
-            rows_copy(twin(d), piece, sibling, pass_send).start()
-    for piece in range(PIECES):
-        rows_copy(sibling, piece, sibling, row_send).wait_recv()
-
-    def add_source(t, totals):
-        x = lax.rem(chip + t // 2, chips) * 2 + lax.rem(core + t, 2)
-
-        @pl.when(jnp.logical_and(lax.rem(t, 2) == 1, t > 1))
-        def _():
-            for piece in range(PIECES):
-                rows_copy(x, piece, sibling, pass_send).wait_recv()
-
+    def add_source(x, totals):
         place = jnp.zeros((n, LANES), jnp.int32)
         offset = jnp.full((n, LANES), -1, jnp.int32)
         for k in range(ranks):
             match = sources[k] == x
             place = jnp.where(match, places[k], place)
             offset = jnp.where(match, offsets[k], offset)
-        offset_of[t] = offset
+        offset_of[x] = offset
         found = offset >= 0
         values = []
         for f in range(26):
             value = jnp.where(found, lane_gather(rows_in[x, f], place), 0.0)
-            rows_of[t, f] = value
+            rows_of[x, f] = value
             values.append(value)
         return tuple(t + v for t, v in zip(totals, normal_rows(values[0:8])))
 
     totals = normal_rows([rows_in[me, f] for f in range(8)])
-    totals = lax.fori_loop(0, n, add_source, tuple(totals))
+    totals = add_source(me, tuple(totals))
+    for piece in range(PIECES):
+        rows_copy(sibling, piece, sibling, row_send).wait_recv()
+    totals = add_source(sibling, totals)
+    for piece in range(PIECES):
+        for d in range(1, chips):
+            rows_copy(twin(d), piece, sibling, row_send).wait_recv()
+            rows_copy(twin(d), piece, sibling, pass_send).start()
+    totals = lax.fori_loop(1, chips, lambda d, t: add_source(twin(d), t), totals)
+
+    def add_passed(d, totals):
+        x = lax.rem(chip + d, chips) * 2 + 1 - core
+        for piece in range(PIECES):
+            rows_copy(x, piece, sibling, pass_send).wait_recv()
+        return add_source(x, totals)
+
+    totals = lax.fori_loop(1, chips, add_passed, totals)
     pivot_one = jnp.sqrt(totals[0] + 1.0)
     inv_one = 1.0 / pivot_one
     low_one = totals[1] * inv_one
@@ -320,7 +342,7 @@
         pair_out_ref[...] += placed[0:81]
         if chunk == last:
             mine_lanes = flipped[:, count * CAM_ROW : (count + 1) * CAM_ROW]
-            hessian_ref[...] = mine_lanes[0:81]
+            hessian_ref[...] = total[:, count * 81 : count * 81 + 81]
             gradient_ref[...] = mine_lanes[81:90]
 
     for d in range(1, n):
@@ -335,6 +357,16 @@
             sum_copy(lax.rem(my_row + d, n_row), my_row, chunk).wait_send()
 
 
+def store_kernel(*refs):
+    copies = [
+        pltpu.make_async_copy(refs[i], refs[3 + i], refs[6].at[i]) for i in range(3)
+    ]
+    for copy in copies:
+        copy.start()
+    for copy in copies:
+        copy.wait()
+
+
 def by_lanes(
     camera_jacobian, point_jacobian, residual, send_order, camera_of, track_of, partner, pair_slot
 ):
@@ -344,18 +376,27 @@
     ranks = partner.shape[0]
     chunks = -(-NBR // PACK)
     vmem = pl.BlockSpec(memory_space=pltpu.VMEM)
+    hbm = pl.BlockSpec(memory_space=pltpu.HBM)
     f32, i32 = jnp.float32, jnp.int32
     dma = pltpu.SemaphoreType.DMA
-    return pl.pallas_call(
+    results = pl.pallas_call(
         functools.partial(step_kernel, n, n_row, cameras),
         out_shape=(
-            jax.ShapeDtypeStruct((81, CAM_ROW), f32),
+            jax.ShapeDtypeStruct((CAM_ROW, 81), f32),
             jax.ShapeDtypeStruct((9, CAM_ROW), f32),
             jax.ShapeDtypeStruct((81, CAM_ROW * NBR), f32),
         ),
-        in_specs=[vmem] * 7,
+        in_specs=[hbm] * 7,
         out_specs=(vmem, vmem, vmem),
         scratch_shapes=[
+            pltpu.VMEM(camera_jacobian.shape, f32),
+            pltpu.VMEM(point_jacobian.shape, f32),
+            pltpu.VMEM(residual.shape, f32),
+            pltpu.VMEM((n, LANES), i32),
+            pltpu.VMEM((n, LANES), i32),
+            pltpu.VMEM(partner.shape, i32),
+            pltpu.VMEM(pair_slot.shape, i32),
+            dma((7,)),
             pltpu.VMEM((n, 26, n, LANES), f32),
             pltpu.VMEM((n * SUBLANES, LANES), i32),
             pltpu.VMEM((n, SUBLANES, LANES), i32),
@@ -391,6 +432,16 @@
         partner,
         pair_slot,
     )
+    hessian, gradient, pair_hessian = pl.pallas_call(
+        store_kernel,
+        out_shape=tuple(jax.ShapeDtypeStruct(r.shape, r.dtype) for r in results),
+        in_specs=[hbm] * 3,
+        out_specs=(hbm,) * 3,
+        scratch_shapes=[dma((3,))],
+        compiler_params=pltpu.CompilerParams(vmem_limit_bytes=VMEM_BYTES),
+        name="store",
+    )(*results)
+    return (hessian.T, gradient, pair_hessian)
 
 
 damping = 1.0

time: 32.6 us -> 30 us (0.920)
  local copies, waits for them, and re-layouts: 7.13 us -> 0 us
  Pallas kernels: 24.4 us -> 29.2 us
    unnamed x16 -> x0, local copies, waits for them, and re-layouts: 6.46 us -> none
    pallas_call x0 -> x1, Pallas kernels: none -> 4.25 us  [by_lanes(): pl.pallas_call(store_kernel, out_shape=tuple((jax.ShapeDtypeStruct(r.shap...]
    pallas_call x1 -> x0, local copies, waits for them, and re-layouts: 0.67 us -> none  [by_lanes(): pl.pallas_call(functools.partial(step_kernel, n, n_row, cameras), out_sha...]
    pallas_call x1, Pallas kernels: 24.4 us -> 24.9 us  [by_lanes(): pl.pallas_call(functools.partial(step_kernel, n, n_row, cameras), out_sha...]
where the time goes in v3:
time: 30 us; the launch traced here: 29.8 us
  Pallas kernels  29.2 us (97%)
  between operations  0.64 us (2%)
    pallas_call x1, Pallas kernels, by_lanes(): pl.pallas_call(functools.partial(step_kernel, n, n_row, cameras), out_sha...  24.9 us
    pallas_call x1, Pallas kernels, by_lanes(): pl.pallas_call(store_kernel, out_shape=tuple((jax.ShapeDtypeStruct(r.shap...  4.25 us

profile of v3, /device:TPU:0, one launch (start us, length us, event | category | flops | bytes accessed | tf_op | source)
XLA Modules:
  0.0 29.8 jit_solution(8708729779945073714)
XLA Ops:
  0.6 24.9 %gauss_newton_step.1 = (f32[16,81]{1,0:T(8,128)}, f32[9,16]{1,0:T(8,128)}, f32[81,224]{1,0:T(8,128)}) custom-call(f32[18,1024]{1,0:T(8,128)} %camera_in.1, f32[6,1024]{1,0:T(8,128)} %point_in.1, f32[2,1024]{1,0:T(2,128)} %resid_in.1, s32[8,128]{1,0:T(8,128)} %bitcast.3, s32[8,128]{1,0:T(8,128)} %bitcast.4, s32[7,1024]{1,0:T(8,128)} %partner_in.1, ...), custom_call_target="tpu_custom_call" | custom-call | tf_op jit(solution)/shard_map/gauss_newton_step/pallas_call | solution.py:382
  25.6 4.2 %store.1 = (f32[16,81]{1,0:T(8,128)}, f32[9,16]{1,0:T(8,128)}, f32[81,224]{1,0:T(8,128)}) custom-call(f32[16,81]{1,0:T(8,128)} %get-tuple-element.9.refs_0_, f32[9,16]{1,0:T(8,128)} %get-tuple-element.10.refs_1_, f32[81,224]{1,0:T(8,128)} %get-tuple-element.11.refs_2_), custom_call_target="tpu_custom_call" | custom-call | tf_op jit(solution)/shard_map/store/pallas_call | solution.py:435

commit v4 on v3

--- a/solution.py
+++ b/solution.py
@@ -358,13 +358,16 @@
 
 
 def store_kernel(*refs):
-    copies = [
-        pltpu.make_async_copy(refs[i], refs[3 + i], refs[6].at[i]) for i in range(3)
-    ]
-    for copy in copies:
-        copy.start()
-    for copy in copies:
-        copy.wait()
+    held, load_sem, store_sem = refs[6:9], refs[9], refs[10]
+    loads = [pltpu.make_async_copy(refs[i], held[i], load_sem.at[i]) for i in range(3)]
+    stores = [pltpu.make_async_copy(held[i], refs[3 + i], store_sem.at[i]) for i in range(3)]
+    for load in loads:
+        load.start()
+    for load, store in zip(loads, stores):
+        load.wait()
+        store.start()
+    for store in stores:
+        store.wait()
 
 
 def by_lanes(
@@ -437,7 +440,7 @@
         out_shape=tuple(jax.ShapeDtypeStruct(r.shape, r.dtype) for r in results),
         in_specs=[hbm] * 3,
         out_specs=(hbm,) * 3,
-        scratch_shapes=[dma((3,))],
+        scratch_shapes=[pltpu.VMEM(r.shape, r.dtype) for r in results] + [dma((3,)), dma((3,))],
         compiler_params=pltpu.CompilerParams(vmem_limit_bytes=VMEM_BYTES),
         name="store",
     )(*results)

time: 30 us -> 27.4 us (0.913)
  Pallas kernels: 29.2 us -> 26.5 us
    pallas_call x1, Pallas kernels: 4.25 us -> 1.61 us  [by_lanes(): pl.pallas_call(store_kernel, out_shape=tuple((jax.ShapeDtypeStruct(r.shap...]
where the time goes in v4:
time: 27.4 us; the launch traced here: 27.2 us
  Pallas kernels  26.5 us (97%)
  between operations  0.64 us (2%)
    pallas_call x1, Pallas kernels, by_lanes(): pl.pallas_call(functools.partial(step_kernel, n, n_row, cameras), out_sha...  24.9 us
    pallas_call x1, Pallas kernels, by_lanes(): pl.pallas_call(store_kernel, out_shape=tuple((jax.ShapeDtypeStruct(r.shap...  1.61 us

profile of v4, /device:TPU:0, one launch (start us, length us, event | category | flops | bytes accessed | tf_op | source)
XLA Modules:
  0.0 27.2 jit_solution(6797952706252972440)
XLA Ops:
  0.6 24.9 %gauss_newton_step.1 = (f32[16,81]{1,0:T(8,128)}, f32[9,16]{1,0:T(8,128)}, f32[81,224]{1,0:T(8,128)}) custom-call(f32[18,1024]{1,0:T(8,128)} %camera_in.1, f32[6,1024]{1,0:T(8,128)} %point_in.1, f32[2,1024]{1,0:T(2,128)} %resid_in.1, s32[8,128]{1,0:T(8,128)} %bitcast.3, s32[8,128]{1,0:T(8,128)} %bitcast.4, s32[7,1024]{1,0:T(8,128)} %partner_in.1, ...), custom_call_target="tpu_custom_call" | custom-call | tf_op jit(solution)/shard_map/gauss_newton_step/pallas_call | solution.py:385
  25.6 1.6 %store.1 = (f32[16,81]{1,0:T(8,128)}, f32[9,16]{1,0:T(8,128)}, f32[81,224]{1,0:T(8,128)}) custom-call(f32[16,81]{1,0:T(8,128)} %get-tuple-element.9.refs_0_, f32[9,16]{1,0:T(8,128)} %get-tuple-element.10.refs_1_, f32[81,224]{1,0:T(8,128)} %get-tuple-element.11.refs_2_), custom_call_target="tpu_custom_call" | custom-call | tf_op jit(solution)/shard_map/store/pallas_call | solution.py:438

commit v5 on v4

--- a/solution.py
+++ b/solution.py
@@ -12,10 +12,19 @@
 LANES = 128
 SUBLANES = 8
 CHUNK = 256
-PACK = 3
-PIECES = 2
 MESH = pl.DeviceIdType.MESH
 VMEM_BYTES = 64 * 1024 * 1024
+
+
+COLUMNS = [[8], [0, 1], [2, 3], [4, 5], [6, 7]]
+PIECES = [
+    [("point", f) for f in range(6)]
+    + [("resid", f) for f in range(2)]
+    + [("camera", 8), ("camera", 17)]
+] + [[("camera", q + 9 * i) for i in range(2) for q in pair] for pair in COLUMNS[1:]]
+TABLE = [entry for piece in PIECES for entry in piece]
+STARTS = [sum(len(piece) for piece in PIECES[:k]) for k in range(len(PIECES))]
+PLACE = {entry: i for i, entry in enumerate(TABLE)}
 
 
 def lane_gather(values, index):
@@ -42,7 +51,8 @@
     camera_in, point_in, resid_in, order_in, ids_in, partner_in, pair_in,
     hessian_ref, gradient_ref, pair_out_ref,
     camera_ref, point_ref, resid_ref, order_ref, ids_ref, partner_ref, pair_ref, load_sem,
-    rows_in, part, staged, pairs, rows_of, offset_of, solve, own, factor_of, prod, marks,
+    rows_in, part, staged, pairs, rows_of, offset_of, place_of, own, normal_of, factor_of, prod,
+    marks,
     partial, landed, turned,
     id_send, id_recv, row_send, row_recv, pass_send, sum_send, sum_recv,
 ):
@@ -54,8 +64,6 @@
     sibling = chip * 2 + 1 - core
     ranks = partner_ref.shape[0]
     shift = LANES.bit_length() - 1
-    size = 26 // PIECES
-    chunks = partial.shape[0]
 
     moves = [
         pltpu.make_async_copy(source, target, load_sem.at[i])
@@ -94,7 +102,7 @@
         )
 
     def rows_copy(source, piece, peer, sem):
-        block = rows_in.at[source, pl.ds(piece * size, size)]
+        block = rows_in.at[source, pl.ds(STARTS[piece], len(PIECES[piece]))]
         return pltpu.make_async_remote_copy(
             src_ref=block,
             dst_ref=block,
@@ -121,13 +129,14 @@
             total = picked if b == 0 else jnp.where(block_of == b, picked, total)
         return total
 
-    table = [(point_ref, f) for f in range(6)] + [(resid_ref, f) for f in range(2)]
-    table = table + [(camera_ref, f) for f in range(18)]
+    inputs = {"point": point_ref, "resid": resid_ref, "camera": camera_ref}
     targets = [twin(d) for d in range(1, chips)] + [sibling]
-    for piece in range(PIECES):
-        for f in range(piece * size, (piece + 1) * size):
-            ref, r = table[f]
-            rows_in[me, f] = permuted(lambda b: ref[r : r + 1, b * LANES : (b + 1) * LANES])
+    for piece in range(len(PIECES)):
+        for i, (name, r) in enumerate(PIECES[piece]):
+            ref = inputs[name]
+            rows_in[me, STARTS[piece] + i] = permuted(
+                lambda b: ref[r : r + 1, b * LANES : (b + 1) * LANES]
+            )
         if piece == 0:
             pl.semaphore_wait(barrier, n - 1 + n_row - 1)
         for peer in targets:
@@ -152,7 +161,6 @@
     for j in range(n):
         pairs[pl.ds(j, ranks, stride=n), :] = pair_ref[:, j * LANES : (j + 1) * LANES]
     turned[...] = jnp.zeros_like(turned)
-    pair_out_ref[...] = jnp.zeros_like(pair_out_ref)
 
     for d in range(1, n):
         peer = lax.rem(me + d, n)
@@ -167,7 +175,7 @@
         places.append(lax.bitwise_and(slot, LANES - 1))
         offsets.append(pair - cam * NBR)
 
-    def add_source(x, totals):
+    def find_partner(x, carry):
         place = jnp.zeros((n, LANES), jnp.int32)
         offset = jnp.full((n, LANES), -1, jnp.int32)
         for k in range(ranks):
@@ -175,32 +183,46 @@
             place = jnp.where(match, places[k], place)
             offset = jnp.where(match, offsets[k], offset)
         offset_of[x] = offset
-        found = offset >= 0
-        values = []
-        for f in range(26):
-            value = jnp.where(found, lane_gather(rows_in[x, f], place), 0.0)
-            rows_of[x, f] = value
-            values.append(value)
-        return tuple(t + v for t, v in zip(totals, normal_rows(values[0:8])))
-
-    totals = normal_rows([rows_in[me, f] for f in range(8)])
-    totals = add_source(me, tuple(totals))
-    for piece in range(PIECES):
-        rows_copy(sibling, piece, sibling, row_send).wait_recv()
-    totals = add_source(sibling, totals)
-    for piece in range(PIECES):
+        place_of[x] = place
+        return carry
+
+    lax.fori_loop(0, n, find_partner, 0)
+
+    def pass_on(piece):
         for d in range(1, chips):
             rows_copy(twin(d), piece, sibling, row_send).wait_recv()
             rows_copy(twin(d), piece, sibling, pass_send).start()
-    totals = lax.fori_loop(1, chips, lambda d, t: add_source(twin(d), t), totals)
-
-    def add_passed(d, totals):
-        x = lax.rem(chip + d, chips) * 2 + 1 - core
-        for piece in range(PIECES):
+
+    def each_source(piece, visit, carry):
+        carry = visit(me, carry)
+        rows_copy(sibling, piece, sibling, row_send).wait_recv()
+        carry = visit(sibling, carry)
+        carry = lax.fori_loop(1, chips, lambda d, c: visit(twin(d), c), carry)
+
+        def passed(d, c):
+            x = lax.rem(chip + d, chips) * 2 + 1 - core
             rows_copy(x, piece, sibling, pass_send).wait_recv()
-        return add_source(x, totals)
-
-    totals = lax.fori_loop(1, chips, add_passed, totals)
+            return visit(x, c)
+
+        return lax.fori_loop(1, chips, passed, carry)
+
+    def gathered(x, piece):
+        place = place_of[x]
+        found = offset_of[x] >= 0
+        return [
+            jnp.where(found, lane_gather(rows_in[x, STARTS[piece] + i], place), 0.0)
+            for i in range(len(PIECES[piece]))
+        ]
+
+    def add_source(x, totals):
+        values = gathered(x, 0)
+        for i, value in enumerate(values):
+            rows_of[x, i] = value
+        return tuple(t + v for t, v in zip(totals, normal_rows(values[0:8])))
+
+    pass_on(0)
+    totals = tuple(normal_rows([rows_in[me, f] for f in range(8)]))
+    totals = each_source(0, add_source, totals)
     pivot_one = jnp.sqrt(totals[0] + 1.0)
     inv_one = 1.0 / pivot_one
     low_one = totals[1] * inv_one
@@ -211,36 +233,29 @@
     h_one = totals[6] * inv_one
     h_two = (totals[7] - low_one * h_one) * inv_two
     h_three = (totals[8] - low_two * h_one - low_mid * h_two) * inv_three
-    for i, value in enumerate([inv_one, low_one, low_two, inv_two, low_mid, inv_three]):
-        solve[i] = value
-
-    def factors(rows):
-        tri = [solve[i] for i in range(6)]
-        columns = []
+
+    def solved(rows):
+        result = []
         for i in range(2):
             jp = [rows(3 * i + c) for c in range(3)]
-            one = jp[0] * tri[0]
-            two = (jp[1] - tri[1] * one) * tri[3]
-            three = (jp[2] - tri[2] * one - tri[4] * two) * tri[5]
-            columns.append((one, two, three))
-        result = [[None] * 9 for _ in range(3)]
-        for p in range(9):
-            first, second = rows(8 + p), rows(17 + p)
-            for c in range(3):
-                result[c][p] = first * columns[0][c] + second * columns[1][c]
+            one = jp[0] * inv_one
+            two = (jp[1] - low_one * one) * inv_two
+            three = (jp[2] - low_two * one - low_mid * two) * inv_three
+            result.append((one, two, three))
         return result
 
-    mine = factors(lambda f: rows_in[me, f])
-    jac = [rows_in[me, 8 + f] for f in range(18)]
+    def put(row, value):
+        prod[pl.ds(pl.multiple_of(row * n, n), n), :] = value
+
+    jac = [rows_in[me, PLACE["camera", f]] for f in range(18)]
+    weight = solved(lambda f: rows_in[me, f])
+    mine = [
+        [jac[p] * weight[0][c] + jac[9 + p] * weight[1][c] for p in range(9)] for c in range(3)
+    ]
     for c in range(3):
         for p in range(9):
             own[c * 9 + p] = -mine[c][p]
-    last = chunks - 1
-    base = last * CHUNK + (NBR - last * PACK) * 81
-
-    def put(row, value):
-        prod[pl.ds(row * n, n), :] = value
-
+    base = NBR * 9
     for p in range(9):
         for q in range(p, 9):
             value = jac[p] * jac[q] + jac[9 + p] * jac[9 + q]
@@ -253,27 +268,16 @@
         back = mine[0][p] * h_one + mine[1][p] * h_two + mine[2][p] * h_three
         put(base + 81 + p, jac[p] * rows_in[me, 6] + jac[9 + p] * rows_in[me, 7] - back)
 
-    def source_factors(x, carry):
-        got = factors(lambda f: rows_of[x, f])
+    def solve_source(x, carry):
+        got = solved(lambda f: rows_of[x, f])
+        for i in range(2):
+            for c in range(3):
+                normal_of[x, 3 * i + c] = got[i][c]
         for c in range(3):
-            for p in range(9):
-                factor_of[x, c * 9 + p] = got[c][p]
+            factor_of[x, c] = rows_of[x, 8] * got[0][c] + rows_of[x, 9] * got[1][c]
         return carry
 
-    lax.fori_loop(0, n, source_factors, 0)
-
-    def at_offset(o, row):
-        picked = [None] * 27
-        for x in range(n):
-            match = offset_of[x] == o
-            for i in range(27):
-                value = jnp.where(match, factor_of[x, i], 0.0)
-                picked[i] = value if x == 0 else picked[i] + value
-        for p in range(9):
-            left = [own[c * 9 + p] for c in range(3)]
-            for q in range(9):
-                value = left[0] * picked[q] + left[1] * picked[9 + q] + left[2] * picked[18 + q]
-                prod[pl.ds(pl.multiple_of((row + 9 * p + q) * n, n), n), :] = value
+    lax.fori_loop(0, n, solve_source, 0)
 
     contract = (((1,), (1,)), ((), ()))
 
@@ -287,17 +291,46 @@
             device_id_type=MESH,
         )
 
-    def chunk_step(chunk, carry):
-        def offset_step(i, inner):
-            at_offset(chunk * PACK + i, chunk * CHUNK + i * 81)
-            return inner
-
-        lax.fori_loop(0, jnp.minimum(PACK, NBR - chunk * PACK), offset_step, 0)
+    for chunk, columns in enumerate(COLUMNS):
+        width = len(columns)
+        if chunk > 0:
+
+            def make_factors(x, carry):
+                values = gathered(x, chunk)
+                for c in range(3):
+                    for i in range(width):
+                        factor_of[x, c * width + i] = (
+                            values[i] * normal_of[x, c] + values[width + i] * normal_of[x, 3 + c]
+                        )
+                return carry
+
+            each_source(chunk, make_factors, 0)
+        if chunk + 1 < len(COLUMNS):
+            pass_on(chunk + 1)
+
+        def at_offset(o, carry):
+            picked = [None] * (3 * width)
+            for x in range(n):
+                match = offset_of[x] == o
+                for i in range(3 * width):
+                    value = jnp.where(match, factor_of[x, i], 0.0)
+                    picked[i] = value if x == 0 else picked[i] + value
+            for p in range(9):
+                left = [own[c * 9 + p] for c in range(3)]
+                for i in range(width):
+                    value = (
+                        left[0] * picked[i]
+                        + left[1] * picked[width + i]
+                        + left[2] * picked[2 * width + i]
+                    )
+                    put(o * (9 * width) + i * 9 + p, value)
+            return carry
+
+        lax.fori_loop(0, NBR, at_offset, 0)
         total = jnp.zeros((cameras, CHUNK), jnp.float32)
         for i in range(n // 2):
-            start = chunk * (CHUNK * n) + 2 * i
-            first = prod[pl.ds(start, CHUNK, stride=n), :]
-            second = prod[pl.ds(start + 1, CHUNK, stride=n), :]
+            first = prod[pl.ds(2 * i, CHUNK, stride=n), :]
+            second = prod[pl.ds(2 * i + 1, CHUNK, stride=n), :]
             both = jnp.concatenate([first, second], axis=1)
             high = both.astype(jnp.bfloat16)
             low = (both - high.astype(jnp.float32)).astype(jnp.bfloat16)
@@ -308,51 +341,46 @@
         partial[chunk] = total
         for d in range(1, n_row):
             sum_copy(lax.rem(my_row + d, n_row), my_row, chunk).start()
-        return carry
-
-    lax.fori_loop(0, chunks, chunk_step, 0)
 
     slots = pair_out_ref.shape[1]
-    lane = lax.broadcasted_iota(jnp.int32, (LANES, slots), 1)
-    line = lax.broadcasted_iota(jnp.int32, (LANES, slots), 0)
-    for chunk in range(chunks):
+    lane = lax.broadcasted_iota(jnp.int32, (slots, slots), 1)
+    line = lax.broadcasted_iota(jnp.int32, (slots, slots), 0)
+    chosen = lane == lax.rem(line, CAM_ROW) * NBR + line // CAM_ROW
+    select = jnp.where(chosen, 1.0, 0.0).astype(jnp.bfloat16)
+    for chunk, columns in enumerate(COLUMNS):
         total = partial[chunk, pl.ds(pl.multiple_of(my_row * CAM_ROW, CAM_ROW), CAM_ROW), :]
         for d in range(1, n_row):
             peer = lax.rem(my_row + d, n_row)
             sum_copy(peer, peer, chunk).wait_recv()
             total = total + landed[peer, chunk]
-        count = min(PACK, NBR - chunk * PACK)
-        for i in range(count):
-            turned[i * CAM_ROW : (i + 1) * CAM_ROW, 0:81] = total[:, i * 81 : (i + 1) * 81]
-        if chunk == last:
-            turned[count * CAM_ROW : (count + 1) * CAM_ROW, 0:90] = total[
-                :, count * 81 : count * 81 + 90
+        height = 9 * len(columns)
+        for o in range(NBR):
+            turned[o * CAM_ROW : (o + 1) * CAM_ROW, 0:height] = total[
+                :, o * height : (o + 1) * height
             ]
         flipped = turned[...].T
-        offset = chunk * PACK + line // CAM_ROW
-        chosen = jnp.logical_and(
-            lane == lax.rem(line, CAM_ROW) * NBR + offset, line < count * CAM_ROW
-        )
-        select = jnp.where(chosen, 1.0, 0.0).astype(jnp.bfloat16)
-        rows = flipped[0:88]
+        rows = flipped[0:24, 0:slots]
         high = rows.astype(jnp.bfloat16)
         low = (rows - high.astype(jnp.float32)).astype(jnp.bfloat16)
         placed = jnp.dot(high, select, preferred_element_type=jnp.float32)
         placed = placed + jnp.dot(low, select, preferred_element_type=jnp.float32)
-        pair_out_ref[...] += placed[0:81]
-        if chunk == last:
-            mine_lanes = flipped[:, count * CAM_ROW : (count + 1) * CAM_ROW]
-            hessian_ref[...] = total[:, count * 81 : count * 81 + 81]
-            gradient_ref[...] = mine_lanes[81:90]
+        for i, q in enumerate(columns):
+            for p in range(9):
+                row = i * 9 + p
+                pair_out_ref[9 * p + q : 9 * p + q + 1, :] = placed[row : row + 1]
+        if chunk == 0:
+            hessian_ref[...] = total[:, base : base + 81]
+            turned[0:CAM_ROW, 0:9] = total[:, base + 81 : base + 90]
+            gradient_ref[...] = turned[0:LANES].T[0:9, 0:CAM_ROW]
 
     for d in range(1, n):
         ids_copy(lax.rem(me + d, n), me).wait_send()
-    for piece in range(PIECES):
+    for piece in range(len(PIECES)):
         for peer in targets:
             rows_copy(me, piece, peer, row_send).wait_send()
         for d in range(1, chips):
             rows_copy(twin(d), piece, sibling, pass_send).wait_send()
-    for chunk in range(chunks):
+    for chunk in range(len(COLUMNS)):
         for d in range(1, n_row):
             sum_copy(lax.rem(my_row + d, n_row), my_row, chunk).wait_send()
 
@@ -377,7 +405,7 @@
     n_row = lax.axis_size("row")
     cameras = CAM_ROW * n_row
     ranks = partner.shape[0]
-    chunks = -(-NBR // PACK)
+    chunks = len(COLUMNS)
     vmem = pl.BlockSpec(memory_space=pltpu.VMEM)
     hbm = pl.BlockSpec(memory_space=pltpu.HBM)
     f32, i32 = jnp.float32, jnp.int32
@@ -404,21 +432,22 @@
             pltpu.VMEM((n * SUBLANES, LANES), i32),
             pltpu.VMEM((n, SUBLANES, LANES), i32),
             pltpu.VMEM((ranks * n, LANES), i32),
-            pltpu.VMEM((n, 26, n, LANES), f32),
+            pltpu.VMEM((n, len(PIECES[0]), n, LANES), f32),
             pltpu.VMEM((n, n, LANES), i32),
-            pltpu.VMEM((6, n, LANES), f32),
+            pltpu.VMEM((n, n, LANES), i32),
             pltpu.VMEM((27, n, LANES), f32),
-            pltpu.VMEM((n, 27, n, LANES), f32),
-            pltpu.VMEM((chunks * CHUNK * n, LANES), f32),
+            pltpu.VMEM((n, 6, n, LANES), f32),
+            pltpu.VMEM((n, 6, n, LANES), f32),
+            pltpu.VMEM((CHUNK * n, LANES), f32),
             pltpu.VMEM((n // 2, cameras, 2 * LANES), jnp.bfloat16),
             pltpu.VMEM((chunks, cameras, CHUNK), f32),
             pltpu.VMEM((n_row, chunks, CAM_ROW, CHUNK), f32),
-            pltpu.VMEM((LANES, LANES), f32),
+            pltpu.VMEM((2 * LANES, LANES), f32),
             dma((n,)),
             dma((n,)),
-            dma((n, PIECES)),
-            dma((n, PIECES)),
-            dma((n, PIECES)),
+            dma((n, len(PIECES))),
+            dma((n, len(PIECES))),
+            dma((n, len(PIECES))),
             dma((n_row, chunks)),
             dma((n_row, chunks)),
         ],

time: 27.4 us -> 28.2 us (1.029)
  Pallas kernels: 26.5 us -> 27.4 us
    pallas_call x1, Pallas kernels: 24.9 us -> 25.7 us  [by_lanes(): pl.pallas_call(functools.partial(step_kernel, n, n_row, cameras), out_sha...]
where the time goes in v5:
time: 28.2 us; the launch traced here: 28 us
  Pallas kernels  27.4 us (97%)
  between operations  0.64 us (2%)
    pallas_call x1, Pallas kernels, by_lanes(): pl.pallas_call(functools.partial(step_kernel, n, n_row, cameras), out_sha...  25.7 us
    pallas_call x1, Pallas kernels, by_lanes(): pl.pallas_call(store_kernel, out_shape=tuple((jax.ShapeDtypeStruct(r.shap...  1.61 us

profile of v5, /device:TPU:0, one launch (start us, length us, event | category | flops | bytes accessed | tf_op | source)
XLA Modules:
  0.0 28.0 jit_solution(16662326417103664824)
XLA Ops:
  0.6 25.7 %gauss_newton_step.1 = (f32[16,81]{1,0:T(8,128)}, f32[9,16]{1,0:T(8,128)}, f32[81,224]{1,0:T(8,128)}) custom-call(f32[18,1024]{1,0:T(8,128)} %camera_in.1, f32[6,1024]{1,0:T(8,128)} %point_in.1, f32[2,1024]{1,0:T(2,128)} %resid_in.1, s32[8,128]{1,0:T(8,128)} %bitcast.3, s32[8,128]{1,0:T(8,128)} %bitcast.4, s32[7,1024]{1,0:T(8,128)} %partner_in.1, ...), custom_call_target="tpu_custom_call" | custom-call | tf_op jit(solution)/shard_map/gauss_newton_step/pallas_call | solution.py:413
  26.4 1.6 %store.1 = (f32[16,81]{1,0:T(8,128)}, f32[9,16]{1,0:T(8,128)}, f32[81,224]{1,0:T(8,128)}) custom-call(f32[16,81]{1,0:T(8,128)} %get-tuple-element.9.refs_0_, f32[9,16]{1,0:T(8,128)} %get-tuple-element.10.refs_1_, f32[81,224]{1,0:T(8,128)} %get-tuple-element.11.refs_2_), custom_call_target="tpu_custom_call" | custom-call | tf_op jit(solution)/shard_map/store/pallas_call | solution.py:467

commit v6 on v5

--- a/solution.py
+++ b/solution.py
@@ -16,12 +16,14 @@
 VMEM_BYTES = 64 * 1024 * 1024
 
 
-COLUMNS = [[8], [0, 1], [2, 3], [4, 5], [6, 7]]
+COLUMNS = [[8], [0, 1, 2, 3], [4, 5, 6, 7]]
 PIECES = [
     [("point", f) for f in range(6)]
     + [("resid", f) for f in range(2)]
     + [("camera", 8), ("camera", 17)]
 ] + [[("camera", q + 9 * i) for i in range(2) for q in pair] for pair in COLUMNS[1:]]
+TERMS = [NBR * 9 * len(columns) + (90 if k == 0 else 0) for k, columns in enumerate(COLUMNS)]
+SIZES = [-(-rows // CHUNK) * CHUNK for rows in TERMS]
 TABLE = [entry for piece in PIECES for entry in piece]
 STARTS = [sum(len(piece) for piece in PIECES[:k]) for k in range(len(PIECES))]
 PLACE = {entry: i for i, entry in enumerate(TABLE)}
@@ -283,8 +285,12 @@
 
     def sum_copy(peer, slot, chunk):
         return pltpu.make_async_remote_copy(
-            src_ref=partial.at[chunk, pl.ds(pl.multiple_of(peer * CAM_ROW, CAM_ROW), CAM_ROW)],
-            dst_ref=landed.at[slot, chunk],
+            src_ref=partial.at[
+                chunk,
+                pl.ds(pl.multiple_of(peer * CAM_ROW, CAM_ROW), CAM_ROW),
+                pl.ds(0, SIZES[chunk]),
+            ],
+            dst_ref=landed.at[slot, chunk, :, pl.ds(0, SIZES[chunk])],
             send_sem=sum_send.at[peer, chunk],
             recv_sem=sum_recv.at[slot, chunk],
             device_id={"row": peer},
@@ -327,18 +333,20 @@
             return carry
 
         lax.fori_loop(0, NBR, at_offset, 0)
-        total = jnp.zeros((cameras, CHUNK), jnp.float32)
-        for i in range(n // 2):
-            first = prod[pl.ds(2 * i, CHUNK, stride=n), :]
-            second = prod[pl.ds(2 * i + 1, CHUNK, stride=n), :]
-            both = jnp.concatenate([first, second], axis=1)
-            high = both.astype(jnp.bfloat16)
-            low = (both - high.astype(jnp.float32)).astype(jnp.bfloat16)
-            for half in (high, low):
-                total += lax.dot_general(
-                    marks[i], half, contract, preferred_element_type=jnp.float32
-                )
-        partial[chunk] = total
+        for part_start in range(0, SIZES[chunk], CHUNK):
+            total = jnp.zeros((cameras, CHUNK), jnp.float32)
+            for i in range(n // 2):
+                start = part_start * n + 2 * i
+                first = prod[pl.ds(start, CHUNK, stride=n), :]
+                second = prod[pl.ds(start + 1, CHUNK, stride=n), :]
+                both = jnp.concatenate([first, second], axis=1)
+                high = both.astype(jnp.bfloat16)
+                low = (both - high.astype(jnp.float32)).astype(jnp.bfloat16)
+                for half in (high, low):
+                    total += lax.dot_general(
+                        marks[i], half, contract, preferred_element_type=jnp.float32
+                    )
+            partial[chunk, :, part_start : part_start + CHUNK] = total
         for d in range(1, n_row):
             sum_copy(lax.rem(my_row + d, n_row), my_row, chunk).start()
 
@@ -348,18 +356,21 @@
     chosen = lane == lax.rem(line, CAM_ROW) * NBR + line // CAM_ROW
     select = jnp.where(chosen, 1.0, 0.0).astype(jnp.bfloat16)
     for chunk, columns in enumerate(COLUMNS):
-        total = partial[chunk, pl.ds(pl.multiple_of(my_row * CAM_ROW, CAM_ROW), CAM_ROW), :]
+        lanes = pl.ds(0, SIZES[chunk])
+        total = partial[
+            chunk, pl.ds(pl.multiple_of(my_row * CAM_ROW, CAM_ROW), CAM_ROW), lanes
+        ]
         for d in range(1, n_row):
             peer = lax.rem(my_row + d, n_row)
             sum_copy(peer, peer, chunk).wait_recv()
-            total = total + landed[peer, chunk]
+            total = total + landed[peer, chunk, :, lanes]
         height = 9 * len(columns)
         for o in range(NBR):
             turned[o * CAM_ROW : (o + 1) * CAM_ROW, 0:height] = total[
                 :, o * height : (o + 1) * height
             ]
         flipped = turned[...].T
-        rows = flipped[0:24, 0:slots]
+        rows = flipped[0 : -(-height // SUBLANES) * SUBLANES, 0:slots]
         high = rows.astype(jnp.bfloat16)
         low = (rows - high.astype(jnp.float32)).astype(jnp.bfloat16)
         placed = jnp.dot(high, select, preferred_element_type=jnp.float32)
@@ -437,11 +448,11 @@
             pltpu.VMEM((n, n, LANES), i32),
             pltpu.VMEM((27, n, LANES), f32),
             pltpu.VMEM((n, 6, n, LANES), f32),
-            pltpu.VMEM((n, 6, n, LANES), f32),
-            pltpu.VMEM((CHUNK * n, LANES), f32),
+            pltpu.VMEM((n, 3 * max(len(c) for c in COLUMNS), n, LANES), f32),
+            pltpu.VMEM((max(SIZES) * n, LANES), f32),
             pltpu.VMEM((n // 2, cameras, 2 * LANES), jnp.bfloat16),
-            pltpu.VMEM((chunks, cameras, CHUNK), f32),
-            pltpu.VMEM((n_row, chunks, CAM_ROW, CHUNK), f32),
+            pltpu.VMEM((chunks, cameras, max(SIZES)), f32),
+            pltpu.VMEM((n_row, chunks, CAM_ROW, max(SIZES)), f32),
             pltpu.VMEM((2 * LANES, LANES), f32),
             dma((n,)),
             dma((n,)),

time: 28.2 us -> 27.1 us (0.961)
  Pallas kernels: 27.4 us -> 26.2 us
    pallas_call x1, Pallas kernels: 25.7 us -> 24.6 us  [by_lanes(): pl.pallas_call(functools.partial(step_kernel, n, n_row, cameras), out_sha...]
where the time goes in v6:
time: 27.1 us; the launch traced here: 26.8 us
  Pallas kernels  26.2 us (97%)
  between operations  0.64 us (2%)
    pallas_call x1, Pallas kernels, by_lanes(): pl.pallas_call(functools.partial(step_kernel, n, n_row, cameras), out_sha...  24.6 us
    pallas_call x1, Pallas kernels, by_lanes(): pl.pallas_call(store_kernel, out_shape=tuple((jax.ShapeDtypeStruct(r.shap...  1.61 us

profile of v6, /device:TPU:0, one launch (start us, length us, event | category | flops | bytes accessed | tf_op | source)
XLA Modules:
  0.0 26.8 jit_solution(5060129375058508589)
XLA Ops:
  0.6 24.6 %gauss_newton_step.1 = (f32[16,81]{1,0:T(8,128)}, f32[9,16]{1,0:T(8,128)}, f32[81,224]{1,0:T(8,128)}) custom-call(f32[18,1024]{1,0:T(8,128)} %camera_in.1, f32[6,1024]{1,0:T(8,128)} %point_in.1, f32[2,1024]{1,0:T(2,128)} %resid_in.1, s32[8,128]{1,0:T(8,128)} %bitcast.3, s32[8,128]{1,0:T(8,128)} %bitcast.4, s32[7,1024]{1,0:T(8,128)} %partner_in.1, ...), custom_call_target="tpu_custom_call" | custom-call | tf_op jit(solution)/shard_map/gauss_newton_step/pallas_call | solution.py:424
  25.2 1.6 %store.1 = (f32[16,81]{1,0:T(8,128)}, f32[9,16]{1,0:T(8,128)}, f32[81,224]{1,0:T(8,128)}) custom-call(f32[16,81]{1,0:T(8,128)} %get-tuple-element.9.refs_0_, f32[9,16]{1,0:T(8,128)} %get-tuple-element.10.refs_1_, f32[81,224]{1,0:T(8,128)} %get-tuple-element.11.refs_2_), custom_call_target="tpu_custom_call" | custom-call | tf_op jit(solution)/shard_map/store/pallas_call | solution.py:478

commit v7 on v6

--- a/solution.py
+++ b/solution.py
@@ -13,7 +13,7 @@
 SUBLANES = 8
 CHUNK = 256
 MESH = pl.DeviceIdType.MESH
-VMEM_BYTES = 64 * 1024 * 1024
+VMEM_BYTES = 32 * 1024 * 1024
 
 
 COLUMNS = [[8], [0, 1, 2, 3], [4, 5, 6, 7]]
@@ -55,7 +55,7 @@
     camera_ref, point_ref, resid_ref, order_ref, ids_ref, partner_ref, pair_ref, load_sem,
     rows_in, part, staged, pairs, rows_of, offset_of, place_of, own, normal_of, factor_of, prod,
     marks,
-    partial, landed, turned,
+    partial, landed, turned, placing,
     id_send, id_recv, row_send, row_recv, pass_send, sum_send, sum_recv,
 ):
     me = lax.axis_index("obs")
@@ -163,6 +163,14 @@
     for j in range(n):
         pairs[pl.ds(j, ranks, stride=n), :] = pair_ref[:, j * LANES : (j + 1) * LANES]
     turned[...] = jnp.zeros_like(turned)
+    slots = pair_out_ref.shape[1]
+    lane = lax.broadcasted_iota(jnp.int32, (slots, slots), 1)
+    line = lax.broadcasted_iota(jnp.int32, (slots, slots), 0)
+    chosen = lane == (
+        lax.bitwise_and(line, CAM_ROW - 1) * NBR
+        + lax.shift_right_logical(line, CAM_ROW.bit_length() - 1)
+    )
+    placing[...] = jnp.where(chosen, 1.0, 0.0).astype(jnp.bfloat16)
 
     for d in range(1, n):
         peer = lax.rem(me + d, n)
@@ -350,11 +358,7 @@
         for d in range(1, n_row):
             sum_copy(lax.rem(my_row + d, n_row), my_row, chunk).start()
 
-    slots = pair_out_ref.shape[1]
-    lane = lax.broadcasted_iota(jnp.int32, (slots, slots), 1)
-    line = lax.broadcasted_iota(jnp.int32, (slots, slots), 0)
-    chosen = lane == lax.rem(line, CAM_ROW) * NBR + line // CAM_ROW
-    select = jnp.where(chosen, 1.0, 0.0).astype(jnp.bfloat16)
+    select = placing[...]
     for chunk, columns in enumerate(COLUMNS):
         lanes = pl.ds(0, SIZES[chunk])
         total = partial[
@@ -397,16 +401,13 @@
 
 
 def store_kernel(*refs):
-    held, load_sem, store_sem = refs[6:9], refs[9], refs[10]
-    loads = [pltpu.make_async_copy(refs[i], held[i], load_sem.at[i]) for i in range(3)]
-    stores = [pltpu.make_async_copy(held[i], refs[3 + i], store_sem.at[i]) for i in range(3)]
-    for load in loads:
-        load.start()
-    for load, store in zip(loads, stores):
-        load.wait()
-        store.start()
-    for store in stores:
-        store.wait()
+    copies = [
+        pltpu.make_async_copy(refs[i], refs[3 + i], refs[6].at[i]) for i in range(3)
+    ]
+    for copy in copies:
+        copy.start()
+    for copy in copies:
+        copy.wait()
 
 
 def by_lanes(
@@ -424,9 +425,9 @@
     results = pl.pallas_call(
         functools.partial(step_kernel, n, n_row, cameras),
         out_shape=(
-            jax.ShapeDtypeStruct((CAM_ROW, 81), f32),
-            jax.ShapeDtypeStruct((9, CAM_ROW), f32),
-            jax.ShapeDtypeStruct((81, CAM_ROW * NBR), f32),
+            pltpu.VMEM((CAM_ROW, 81), f32),
+            pltpu.VMEM((9, CAM_ROW), f32),
+            pltpu.VMEM((81, CAM_ROW * NBR), f32),
         ),
         in_specs=[hbm] * 7,
         out_specs=(vmem, vmem, vmem),
@@ -454,6 +455,7 @@
             pltpu.VMEM((chunks, cameras, max(SIZES)), f32),
             pltpu.VMEM((n_row, chunks, CAM_ROW, max(SIZES)), f32),
             pltpu.VMEM((2 * LANES, LANES), f32),
+            pltpu.VMEM((CAM_ROW * NBR, CAM_ROW * NBR), jnp.bfloat16),
             dma((n,)),
             dma((n,)),
             dma((n, len(PIECES))),
@@ -467,21 +469,25 @@
         ),
         name="gauss_newton_step",
     )(
-        camera_jacobian,
-        point_jacobian,
-        residual,
-        send_order.reshape(n, LANES),
-        camera_of.reshape(n, LANES),
-        partner,
-        pair_slot,
+        *(
+            pltpu.with_memory_space_constraint(value, pltpu.HBM)
+            for value in (
+                camera_jacobian,
+                point_jacobian,
+                residual,
+                send_order.reshape(n, LANES),
+                camera_of.reshape(n, LANES),
+                partner,
+                pair_slot,
+            )
+        )
     )
     hessian, gradient, pair_hessian = pl.pallas_call(
         store_kernel,
-        out_shape=tuple(jax.ShapeDtypeStruct(r.shape, r.dtype) for r in results),
-        in_specs=[hbm] * 3,
+        out_shape=tuple(pltpu.HBM(r.shape, r.dtype) for r in results),
+        in_specs=[vmem] * 3,
         out_specs=(hbm,) * 3,
-        scratch_shapes=[pltpu.VMEM(r.shape, r.dtype) for r in results] + [dma((3,)), dma((3,))],
-        compiler_params=pltpu.CompilerParams(vmem_limit_bytes=VMEM_BYTES),
+        scratch_shapes=[dma((3,))],
         name="store",
     )(*results)
     return (hessian.T, gradient, pair_hessian)

time: 27.1 us -> 28.2 us (1.041)
  local copies, waits for them, and re-layouts: 0 us -> 1.81 us
  Pallas kernels: 26.2 us -> 25.5 us
    unnamed x0 -> x6, local copies, waits for them, and re-layouts: none -> 1.81 us
    pallas_call x1, Pallas kernels: 24.6 us -> 24 us  [by_lanes(): pl.pallas_call(functools.partial(step_kernel, n, n_row, cameras), out_sha...]
where the time goes in v7:
time: 28.2 us; the launch traced here: 28 us
  Pallas kernels  25.5 us (90%)
  local copies, waits for them, and re-layouts  1.81 us (6%)
  between operations  0.65 us (2%)
    pallas_call x1, Pallas kernels, by_lanes(): pl.pallas_call(functools.partial(step_kernel, n, n_row, cameras), out_sha...  24 us
    unnamed x6, local copies, waits for them, and re-layouts  1.81 us
    pallas_call x1, Pallas kernels, by_lanes(): pl.pallas_call(store_kernel, out_shape=tuple((pltpu.HBM(r.shape, r.dtype)...  1.59 us

profile of v7, /device:TPU:0, one launch (start us, length us, event | category | flops | bytes accessed | tf_op | source)
XLA Modules:
  0.0 28.0 jit_solution(4497607311107488136)
XLA Ops:
  0.6 24.0 %gauss_newton_step.1 = (f32[16,81]{1,0:T(8,128)S(1)}, f32[9,16]{1,0:T(8,128)S(1)}, f32[81,224]{1,0:T(8,128)S(1)}) custom-call(f32[18,1024]{1,0:T(8,128)} %camera_in.1, f32[6,1024]{1,0:T(8,128)} %point_in.1, f32[2,1024]{1,0:T(2,128)} %resid_in.1, s32[8,128]{1,0:T(8,128)} %bitcast.3, s32[8,128]{1,0:T(8,128)} %bitcast.4, s32[7,1024]{1,0:T(8,128)} %partner_in.1, ...), custom_call_target="tpu_custom_call" | custom-call | tf_op jit(solution)/shard_map/gauss_newton_step/pallas_call | solution.py:425
  24.6 0.0 copy-start
  24.6 0.6 %copy-done = f32[81,224]{1,0:T(8,128)} copy-done((f32[81,224]{1,0:T(8,128)}, f32[81,224]{1,0:T(8,128)S(1)}, u32[]{:S(2)}) %copy-start) | copy-done | bytes 72600
  25.2 0.0 copy-start.1
  25.2 0.6 %copy-done.1 = f32[16,81]{1,0:T(8,128)} copy-done((f32[16,81]{1,0:T(8,128)}, f32[16,81]{1,0:T(8,128)S(1)}, u32[]{:S(2)}) %copy-start.1) | copy-done | bytes 5208
  25.8 0.0 copy-start.2
  25.8 0.6 %copy-done.2 = f32[9,16]{1,0:T(8,128)} copy-done((f32[9,16]{1,0:T(8,128)}, f32[9,16]{1,0:T(8,128)S(1)}, u32[]{:S(2)}) %copy-start.2) | copy-done | bytes 600
  26.4 1.6 %store.1 = (f32[16,81]{1,0:T(8,128)}, f32[9,16]{1,0:T(8,128)}, f32[81,224]{1,0:T(8,128)}) custom-call(f32[16,81]{1,0:T(8,128)} %copy-done.1, f32[9,16]{1,0:T(8,128)} %copy-done.2, f32[81,224]{1,0:T(8,128)} %copy-done), custom_call_target="tpu_custom_call" | custom-call | tf_op jit(solution)/shard_map/store/pallas_call | solution.py:485
Async XLA Ops:
  24.6 0.6 %copy-start = (f32[81,224]{1,0:T(8,128)}, f32[81,224]{1,0:T(8,128)S(1)}, u32[]{:S(2)}) copy-start(f32[81,224]{1,0:T(8,128)S(1)} %get-tuple-element.11.refs_2_) | copy-start | bytes 217732
  25.2 0.6 %copy-start.1 = (f32[16,81]{1,0:T(8,128)}, f32[16,81]{1,0:T(8,128)S(1)}, u32[]{:S(2)}) copy-start(f32[16,81]{1,0:T(8,128)S(1)} %get-tuple-element.9.refs_0_) | copy-start | bytes 15556
  25.8 0.6 %copy-start.2 = (f32[9,16]{1,0:T(8,128)}, f32[9,16]{1,0:T(8,128)S(1)}, u32[]{:S(2)}) copy-start(f32[9,16]{1,0:T(8,128)S(1)} %get-tuple-element.10.refs_1_) | copy-start | bytes 1732

commit v8 on v7

--- a/solution.py
+++ b/solution.py
@@ -488,8 +488,9 @@
         in_specs=[vmem] * 3,
         out_specs=(hbm,) * 3,
         scratch_shapes=[dma((3,))],
+        compiler_params=pltpu.CompilerParams(vmem_limit_bytes=4 * 1024 * 1024),
         name="store",
-    )(*results)
+    )(*(pltpu.with_memory_space_constraint(r, pltpu.VMEM) for r in results))
     return (hessian.T, gradient, pair_hessian)
 
 

time: 28.2 us -> 25.4 us (0.901)
  local copies, waits for them, and re-layouts: 1.81 us -> 0 us
  Pallas kernels: 25.5 us -> 24.6 us
    unnamed x6 -> x0, local copies, waits for them, and re-layouts: 1.81 us -> none
    pallas_call x1, Pallas kernels: 1.59 us -> 0.67 us  [by_lanes(): pl.pallas_call(store_kernel, out_shape=tuple((pltpu.HBM(r.shape, r.dtype)...]
where the time goes in v8:
time: 25.4 us; the launch traced here: 25.3 us
  Pallas kernels  24.6 us (97%)
  between operations  0.64 us (3%)
    pallas_call x1, Pallas kernels, by_lanes(): pl.pallas_call(functools.partial(step_kernel, n, n_row, cameras), out_sha...  24 us
    pallas_call x1, Pallas kernels, by_lanes(): pl.pallas_call(store_kernel, out_shape=tuple((pltpu.HBM(r.shape, r.dtype)...  0.67 us

profile of v8, /device:TPU:0, one launch (start us, length us, event | category | flops | bytes accessed | tf_op | source)
XLA Modules:
  0.0 25.3 jit_solution(13952426728401488364)
XLA Ops:
  0.6 24.0 %gauss_newton_step.1 = (f32[16,81]{1,0:T(8,128)S(1)}, f32[9,16]{1,0:T(8,128)S(1)}, f32[81,224]{1,0:T(8,128)S(1)}) custom-call(f32[18,1024]{1,0:T(8,128)} %camera_in.1, f32[6,1024]{1,0:T(8,128)} %point_in.1, f32[2,1024]{1,0:T(2,128)} %resid_in.1, s32[8,128]{1,0:T(8,128)} %bitcast.3, s32[8,128]{1,0:T(8,128)} %bitcast.4, s32[7,1024]{1,0:T(8,128)} %partner_in.1, ...), custom_call_target="tpu_custom_call" | custom-call | tf_op jit(solution)/shard_map/gauss_newton_step/pallas_call | solution.py:425
  24.6 0.7 %store.1 = (f32[16,81]{1,0:T(8,128)}, f32[9,16]{1,0:T(8,128)}, f32[81,224]{1,0:T(8,128)}) custom-call(f32[16,81]{1,0:T(8,128)S(1)} %get-tuple-element.9.refs_0_, f32[9,16]{1,0:T(8,128)S(1)} %get-tuple-element.10.refs_1_, f32[81,224]{1,0:T(8,128)S(1)} %get-tuple-element.11.refs_2_), custom_call_target="tpu_custom_call" | custom-call | tf_op jit(solution)/shard_map/store/pallas_call | solution.py:485
